TPU v7x, 128 devices: a whole 4x4x4 slice. The times are simulated.
128 devices in a mesh: seq: 8 (over z, x_lo), head: 16 (over x_hi, y, core).
Axes of the slice: x: 4 (x_hi: 2, x_lo: 2; x = x_hi * 2 + x_lo), y: 4, z: 4, core: 2. Of those that a mesh axis runs over, the one named last changes fastest.
Arguments:
- query_rows: bfloat16 [2, 4096, 64, 128], P(None, 'seq', 'head'), may hold values from -96 to 96
- key_rows: bfloat16 [2, 4096, 8, 128], P(None, 'seq'), may hold values from -4 to 4
- value_rows: bfloat16 [2, 4096, 8, 128], P(None, 'seq'), may hold values from -6 to 6
- state_in: bfloat16 [2, 4096, 8, 128], P(None, 'seq'), may hold values from -0.44921875 to 0.44921875
- state_out: bfloat16 [2, 4096, 8, 128], P(None, 'seq'), may hold values from -0.44921875 to 0.44921875
- log_decay: float32 [2, 64, 4096], P(None, 'head', 'seq'), may hold values from -0.75 to 0
- doc_ids: int32 [2, 4096], P(None, 'seq'), may hold values from 0 to 3, never falling along the last dimension, each value on 1 to 2048 neighbouring positions
- norm_gain: float32 [8192], replicated, may hold values from 0.1 to 1.9
Outputs:
- hidden_gap: bfloat16 [2, 4096, 8192], P(None, ('seq', 'head'))
- align_err: float32 [2, 64, 4096], P(None, 'head', 'seq')
Inputs may be any that keep to these rules, and one draw needn't show every extreme that they name: `doc_ids`: within each sequence the ids never fall, each document spans 1 to 2048 positions and one spans exactly 2048.
All inputs are finite; a program needn't handle non-finite values.
Results may differ from a plain program's by a relative error of at most 0.0065.
Values may be sent and summed in bfloat16 or wider, within the bound.
A program may use at most 64 MiB of HBM per device.

v0:
```python
import math

import jax
import jax.numpy as jnp
from jax import lax
from jax.sharding import PartitionSpec as P

HEAD_COUNT = 64
KVH = 8


NEG_FILL = -1e30
EPS = 1e-05


def normalize(teach, stud, gain, width_all):
    teach_f = teach.astype(jnp.float32)
    stud_f = stud.astype(jnp.float32)
    teach_ms = jnp.sum(teach_f * teach_f, axis=-1, keepdims=True) / width_all + EPS
    stud_ms = jnp.sum(stud_f * stud_f, axis=-1, keepdims=True) / width_all + EPS
    return (gain * stud_f * lax.rsqrt(stud_ms) - teach_f * lax.rsqrt(teach_ms)).astype(jnp.bfloat16)


def make_state(seqs_here, heads_dev, row_count, head_size):
    row_shape = (seqs_here, heads_dev, row_count)
    acc_shape = (seqs_here, row_count, heads_dev, head_size)
    return (
        jnp.full(row_shape, NEG_FILL, jnp.float32),
        jnp.zeros(row_shape, jnp.float32),
        jnp.zeros(row_shape, jnp.float32),
        jnp.zeros(row_shape, jnp.float32),
        jnp.zeros(row_shape, jnp.float32),
        jnp.zeros(acc_shape, jnp.float32),
        jnp.zeros(acc_shape, jnp.float32),
    )


def on_device(query_rows, key_rows, value_rows, state_in, state_out, log_decay, doc_ids, norm_gain):
    seqs_here, stretch, heads_dev, head_size = query_rows.shape
    group = HEAD_COUNT // KVH
    scale = 1.0 / math.sqrt(head_size)
    head_pos = lax.axis_index("head")
    owner = head_pos * heads_dev // group
    key_own = lax.dynamic_index_in_dim(key_rows, owner, 2, keepdims=False)
    value_own = lax.dynamic_index_in_dim(value_rows, owner, 2, keepdims=False)
    inner_own = lax.dynamic_index_in_dim(state_in, owner, 2, keepdims=False)
    outer_own = lax.dynamic_index_in_dim(state_out, owner, 2, keepdims=False)
    decay_all, docs_float = (
        lax.all_gather(log_decay, "seq", axis=2, tiled=True),
        lax.all_gather(doc_ids.astype(jnp.float32), "seq", axis=1, tiled=True),
    )
    docs_all = docs_float.astype(jnp.int32)
    cum_all = jnp.cumsum(decay_all, axis=2)
    seq_pos = lax.axis_index("seq")
    first = seq_pos * stretch
    cum_query = lax.dynamic_slice_in_dim(cum_all, first, stretch, 2)
    query_pos = first + jnp.arange(stretch, dtype=jnp.int32)

    def tile(carry, block, kstart, queries):
        query, outer, qpos, qdoc, cumq = queries
        key_blk, value_blk, inner_blk = block
        width = key_blk.shape[1]
        key_pos = kstart + jnp.arange(width, dtype=jnp.int32)
        doc_key = lax.dynamic_slice_in_dim(docs_all, kstart, width, 1)
        cum_key = lax.dynamic_slice_in_dim(cum_all, kstart, width, 2)
        causal = (qpos[:, None] >= key_pos[None, :])[None, None]
        same_doc = qdoc[:, None, :, None] == doc_key[:, None, None, :]
        visible = causal & same_doc
        best, total, cross, square, mixsq, out_acc, mix_acc = carry
        scores = (
            jnp.einsum("sqhd,skd->shqk", query, key_blk, preferred_element_type=jnp.float32) * scale
        )
        top = jnp.maximum(best, jnp.max(jnp.where(visible, scores, NEG_FILL), axis=-1))
        factor = jnp.exp(best - top)
        weights = jnp.where(visible, jnp.exp(scores - top[..., None]), 0.0)
        inner = jnp.einsum("sqn,skn->sqk", outer, inner_blk, preferred_element_type=jnp.float32)
        decay = jnp.exp(jnp.where(visible, cumq[..., None] - cum_key[:, :, None, :], NEG_FILL))
        mixing = decay * inner[:, None]
        total = total * factor + jnp.sum(weights, axis=-1)
        cross = cross * factor + jnp.sum(mixing * weights, axis=-1)
        square = square * factor * factor + jnp.sum(weights * weights, axis=-1)
        mixsq = mixsq + jnp.sum(mixing * mixing, axis=-1)
        factor_rows = jnp.transpose(factor, (0, 2, 1))[..., None]
        out_acc = out_acc * factor_rows + jnp.einsum(
            "shqk,skd->sqhd",
            weights.astype(jnp.bfloat16),
            value_blk,
            preferred_element_type=jnp.float32,
        )
        mix_acc = mix_acc + jnp.einsum(
            "shqk,skd->sqhd",
            mixing.astype(jnp.bfloat16),
            value_blk,
            preferred_element_type=jnp.float32,
        )
        return (top, total, cross, square, mixsq, out_acc, mix_acc)

    own_queries = (query_rows, outer_own, query_pos, doc_ids, cum_query)
    start_value = make_state(seqs_here, heads_dev, stretch, head_size)
    piece = (
        lax.all_gather(key_own, "seq", axis=1, tiled=True),
        lax.all_gather(value_own, "seq", axis=1, tiled=True),
        lax.all_gather(inner_own, "seq", axis=1, tiled=True),
    )
    width = piece[0].shape[1]
    step = math.gcd(width, 512)
    count = width // step

    def advance(index, state):
        offset = index * step
        block = tuple((lax.dynamic_slice_in_dim(member, offset, step, 1) for member in piece))
        return tile(state, block, offset, own_queries)

    folded = lax.fori_loop(0, count, advance, start_value)
    best, total, cross, square, mixsq, out_acc, mix_acc = folded
    error_rows = mixsq - 2.0 * cross / total + square / (total * total)
    total_rows = jnp.transpose(total, (0, 2, 1))[..., None]
    row_width = heads_dev * head_size
    teach_rows = (out_acc / total_rows).astype(jnp.bfloat16).reshape(seqs_here, stretch, row_width)
    stud_rows = mix_acc.astype(jnp.bfloat16).reshape(seqs_here, stretch, row_width)
    width = heads_dev * head_size
    width_all = width * lax.axis_size("head")
    hidden_gap = normalize(
        lax.all_to_all(teach_rows, "head", split_axis=1, concat_axis=2, tiled=True),
        lax.all_to_all(stud_rows, "head", split_axis=1, concat_axis=2, tiled=True),
        norm_gain,
        width_all,
    )
    return (hidden_gap, error_rows)


def solution(mesh):
    placed = (
        P(None, "seq", "head", None),
        P(None, "seq", None, None),
        P(None, "seq", None, None),
        P(None, "seq", None, None),
        P(None, "seq", None, None),
        P(None, "head", "seq"),
        P(None, "seq"),
        P(),
    )
    return jax.shard_map(
        on_device,
        mesh=mesh,
        in_specs=placed,
        out_specs=(P(None, ("seq", "head"), None), P(None, "head", "seq")),
        check_vma=False,
    )
```

profile of v0, /device:TPU:89, one launch (start us, length us, event | category | flops | bytes accessed | tf_op | source)
XLA Modules:
  0.0 397.0 jit_solution(11302896038608791161)
XLA Ops:
  16.4 20.3 %all_gather.15 = f32[2,4096]{1,0:T(2,128)S(1)} all-gather(f32[2,512]{1,0:T(2,128)S(1)} %convert_element_type.63), channel_id=1, replica_groups=mesh['seq'=8,'head'=16] {'seq'}, dimensions={1}, use_global_device_ids=true | all-gather | bytes 36864 | tf_op jit(solution)/shard_map/all_gather | solution.py:50
  36.7 24.5 %all_gather.17 = f32[2,4,4096]{2,1,0:T(4,128)S(1)} all-gather(f32[2,4,512]{2,1,0:T(4,128)S(1)} %copy-done.9), channel_id=1, replica_groups=mesh['seq'=8,'head'=16] {'seq'}, dimensions={2}, use_global_device_ids=true | all-gather | bytes 147456 | tf_op jit(solution)/shard_map/all_gather | solution.py:49
  69.3 48.3 %all-gather.11.cloned.1.call-done = bf16[2,4096,1,128]{1,3,0,2:T(8,128)(2,1)} async-done(((bf16[2,512,1,128]{1,3,0,2:T(8,128)(2,1)}), bf16[2,4096,1,128]{1,3,0,2:T(8,128)(2,1)}) %all-gather.11.cloned.1.call-update) | async-done | bytes 2097168 | tf_op jit(solution)/shard_map/all_gather | solution.py:102
  117.7 53.2 %all-gather.9.cloned.1.call-done = bf16[2,4096,1,128]{3,1,0,2:T(8,128)(2,1)} async-done(((bf16[2,512,1,128]{3,1,0,2:T(8,128)(2,1)}), bf16[2,4096,1,128]{3,1,0,2:T(8,128)(2,1)}) %all-gather.9.cloned.1.call-update) | async-done | bytes 2097168 | tf_op jit(solution)/shard_map/all_gather | solution.py:103
  170.9 165.7 %while.26 = (s32[]{:T(128)}, f32[2,4,512]{2,1,0:T(4,128)S(1)}, f32[2,4,512]{2,1,0:T(4,128)S(1)}, f32[2,4,512]{2,1,0:T(4,128)S(1)}, f32[2,4,512]{2,1,0:T(4,128)S(...) while((s32[]{:T(128)}, f32[2,4,512]{2,1,0:T(4,128)S(1)}, ...), condition=%wide.region_8.9_spmd.clone, body=%wide.region_2.0_spmd.clone.sunk | while | flops 1799140352 | bytes 79503760 | solution.py:114
  180.6 6.2 %multiply_reduce_fusion.6 = (f32[2,4,512]{2,1,0:T(4,128)S(1)}, f32[2,4,512]{2,1,0:T(4,128)S(1)}, f32[2,4,512]{2,1,0:T(4,128)S(1)}, f32[2,4,512]{2,1,0:T(4,128)S(1)}) fusion(f32[2,4,512]{2,1,0:T(4,128)S(1)} %select_maximum_fusion.2, f32[2,512,512,4]{2,1,3,0:T(8,128)S(1)} %get-tuple-element.622, pred[2,512,512]{1,2,0:T(8,128)(4,1)S(1)} %compare_and_fusion.2, ...), kind=kLoop, calls=%fused_computation.7.clone.1 | loop fusion | flops 27246592 | bytes 11124736 | tf_op jit(solution)/shard_map/while/body/eval_jaxpr/reduce_sum | solution.py:81
  194.5 4.0 bitcast_add_fusion.5
  201.3 6.2 %multiply_reduce_fusion.6 = (f32[2,4,512]{2,1,0:T(4,128)S(1)}, f32[2,4,512]{2,1,0:T(4,128)S(1)}, f32[2,4,512]{2,1,0:T(4,128)S(1)}, f32[2,4,512]{2,1,0:T(4,128)S(1)}) fusion(f32[2,4,512]{2,1,0:T(4,128)S(1)} %select_maximum_fusion.2, f32[2,512,512,4]{2,1,3,0:T(8,128)S(1)} %get-tuple-element.622, pred[2,512,512]{1,2,0:T(8,128)(4,1)S(1)} %compare_and_fusion.2, ...), kind=kLoop, calls=%fused_computation.7.clone.1 | loop fusion | flops 27246592 | bytes 11124736 | tf_op jit(solution)/shard_map/while/body/eval_jaxpr/reduce_sum | solution.py:81
  215.3 4.0 bitcast_add_fusion.5
  222.1 6.2 %multiply_reduce_fusion.6 = (f32[2,4,512]{2,1,0:T(4,128)S(1)}, f32[2,4,512]{2,1,0:T(4,128)S(1)}, f32[2,4,512]{2,1,0:T(4,128)S(1)}, f32[2,4,512]{2,1,0:T(4,128)S(1)}) fusion(f32[2,4,512]{2,1,0:T(4,128)S(1)} %select_maximum_fusion.2, f32[2,512,512,4]{2,1,3,0:T(8,128)S(1)} %get-tuple-element.622, pred[2,512,512]{1,2,0:T(8,128)(4,1)S(1)} %compare_and_fusion.2, ...), kind=kLoop, calls=%fused_computation.7.clone.1 | loop fusion | flops 27246592 | bytes 11124736 | tf_op jit(solution)/shard_map/while/body/eval_jaxpr/reduce_sum | solution.py:81
  236.0 4.0 bitcast_add_fusion.5
  242.8 6.2 %multiply_reduce_fusion.6 = (f32[2,4,512]{2,1,0:T(4,128)S(1)}, f32[2,4,512]{2,1,0:T(4,128)S(1)}, f32[2,4,512]{2,1,0:T(4,128)S(1)}, f32[2,4,512]{2,1,0:T(4,128)S(1)}) fusion(f32[2,4,512]{2,1,0:T(4,128)S(1)} %select_maximum_fusion.2, f32[2,512,512,4]{2,1,3,0:T(8,128)S(1)} %get-tuple-element.622, pred[2,512,512]{1,2,0:T(8,128)(4,1)S(1)} %compare_and_fusion.2, ...), kind=kLoop, calls=%fused_computation.7.clone.1 | loop fusion | flops 27246592 | bytes 11124736 | tf_op jit(solution)/shard_map/while/body/eval_jaxpr/reduce_sum | solution.py:81
  256.7 4.0 bitcast_add_fusion.5
  263.5 6.2 %multiply_reduce_fusion.6 = (f32[2,4,512]{2,1,0:T(4,128)S(1)}, f32[2,4,512]{2,1,0:T(4,128)S(1)}, f32[2,4,512]{2,1,0:T(4,128)S(1)}, f32[2,4,512]{2,1,0:T(4,128)S(1)}) fusion(f32[2,4,512]{2,1,0:T(4,128)S(1)} %select_maximum_fusion.2, f32[2,512,512,4]{2,1,3,0:T(8,128)S(1)} %get-tuple-element.622, pred[2,512,512]{1,2,0:T(8,128)(4,1)S(1)} %compare_and_fusion.2, ...), kind=kLoop, calls=%fused_computation.7.clone.1 | loop fusion | flops 27246592 | bytes 11124736 | tf_op jit(solution)/shard_map/while/body/eval_jaxpr/reduce_sum | solution.py:81
  277.4 4.0 bitcast_add_fusion.5
  284.2 6.2 %multiply_reduce_fusion.6 = (f32[2,4,512]{2,1,0:T(4,128)S(1)}, f32[2,4,512]{2,1,0:T(4,128)S(1)}, f32[2,4,512]{2,1,0:T(4,128)S(1)}, f32[2,4,512]{2,1,0:T(4,128)S(1)}) fusion(f32[2,4,512]{2,1,0:T(4,128)S(1)} %select_maximum_fusion.2, f32[2,512,512,4]{2,1,3,0:T(8,128)S(1)} %get-tuple-element.622, pred[2,512,512]{1,2,0:T(8,128)(4,1)S(1)} %compare_and_fusion.2, ...), kind=kLoop, calls=%fused_computation.7.clone.1 | loop fusion | flops 27246592 | bytes 11124736 | tf_op jit(solution)/shard_map/while/body/eval_jaxpr/reduce_sum | solution.py:81
  298.1 4.0 bitcast_add_fusion.5
  304.9 6.2 %multiply_reduce_fusion.6 = (f32[2,4,512]{2,1,0:T(4,128)S(1)}, f32[2,4,512]{2,1,0:T(4,128)S(1)}, f32[2,4,512]{2,1,0:T(4,128)S(1)}, f32[2,4,512]{2,1,0:T(4,128)S(1)}) fusion(f32[2,4,512]{2,1,0:T(4,128)S(1)} %select_maximum_fusion.2, f32[2,512,512,4]{2,1,3,0:T(8,128)S(1)} %get-tuple-element.622, pred[2,512,512]{1,2,0:T(8,128)(4,1)S(1)} %compare_and_fusion.2, ...), kind=kLoop, calls=%fused_computation.7.clone.1 | loop fusion | flops 27246592 | bytes 11124736 | tf_op jit(solution)/shard_map/while/body/eval_jaxpr/reduce_sum | solution.py:81
  318.8 4.0 bitcast_add_fusion.5
  325.6 6.2 %multiply_reduce_fusion.6 = (f32[2,4,512]{2,1,0:T(4,128)S(1)}, f32[2,4,512]{2,1,0:T(4,128)S(1)}, f32[2,4,512]{2,1,0:T(4,128)S(1)}, f32[2,4,512]{2,1,0:T(4,128)S(1)}) fusion(f32[2,4,512]{2,1,0:T(4,128)S(1)} %select_maximum_fusion.2, f32[2,512,512,4]{2,1,3,0:T(8,128)S(1)} %get-tuple-element.622, pred[2,512,512]{1,2,0:T(8,128)(4,1)S(1)} %compare_and_fusion.2, ...), kind=kLoop, calls=%fused_computation.7.clone.1 | loop fusion | flops 27246592 | bytes 11124736 | tf_op jit(solution)/shard_map/while/body/eval_jaxpr/reduce_sum | solution.py:81
  340.5 7.2 %all-to-all-start.1 = ((bf16[2,512,512]{2,0,1:T(2,128)(2,1)}), bf16[2,512,512]{2,0,1:T(2,128)(2,1)S(1)}, u32[]{:S(2)}, u32[]{:S(2)}) async-start(bf16[2,512,512]{2,0,1:T(2,128)(2,1)} %copy.67), calls=%async_computation.1 | async-start | bytes 2097152 | tf_op jit(solution)/shard_map/all_to_all | solution.py:124
  354.2 10.0 %all-to-all-done.1 = bf16[2,512,512]{2,0,1:T(2,128)(2,1)S(1)} async-done(((bf16[2,512,512]{2,0,1:T(2,128)(2,1)}), bf16[2,512,512]{2,0,1:T(2,128)(2,1)S(1)}, u32[]{:S(2)}, u32[]{:S(2)}) %all-to-all-start.1) | async-done | bytes 1048608 | tf_op jit(solution)/shard_map/all_to_all | solution.py:124
  365.2 5.1 %all-to-all-start = ((bf16[2,512,512]{2,0,1:T(2,128)(2,1)}), bf16[2,512,512]{2,0,1:T(2,128)(2,1)S(1)}, u32[]{:S(2)}, u32[]{:S(2)}) async-start(bf16[2,512,512]{2,0,1:T(2,128)(2,1)} %copy.66), calls=%async_computation | async-start | bytes 2097152 | tf_op jit(solution)/shard_map/all_to_all | solution.py:125
  375.7 11.1 %all-to-all-done = bf16[2,512,512]{2,0,1:T(2,128)(2,1)S(1)} async-done(((bf16[2,512,512]{2,0,1:T(2,128)(2,1)}), bf16[2,512,512]{2,0,1:T(2,128)(2,1)S(1)}, u32[]{:S(2)}, u32[]{:S(2)}) %all-to-all-start) | async-done | bytes 1048608 | tf_op jit(solution)/shard_map/all_to_all | solution.py:125
  (230 shorter events, 125.2 us)
Async XLA Ops:
  7.2 62.1 %all-gather.7.cloned.1.call-start = ((), (), s32[]{:S(2)}) async-start(), calls=%async_computation.2 | async-start | bytes 2359296 | tf_op jit(solution)/shard_map/all_gather | solution.py:101
  10.1 6.3 %copy-start.7 = (s32[2,512]{1,0:T(2,128)S(1)}, s32[2,512]{1,0:T(2,128)}, u32[]{:S(2)}) copy-start(s32[2,512]{1,0:T(2,128)} %param.16) | copy-start | bytes 12292
  10.1 26.6 %copy-start.9 = (f32[2,4,512]{2,1,0:T(4,128)S(1)}, f32[2,4,512]{2,1,0:T(4,128)}, u32[]{:S(2)}) copy-start(f32[2,4,512]{2,1,0:T(4,128)} %param.15) | copy-start | bytes 49156
  10.1 107.6 %all-gather.11.cloned.1.call-start = ((), (), s32[]{:S(2)}) async-start(), calls=%async_computation.4 | async-start | bytes 2359296 | tf_op jit(solution)/shard_map/all_gather | solution.py:102
  13.3 157.6 %all-gather.9.cloned.1.call-start = ((), (), s32[]{:S(2)}) async-start(), calls=%async_computation.3 | async-start | bytes 2359296 | tf_op jit(solution)/shard_map/all_gather | solution.py:103
  170.9 3.0 copy-start.3
  180.6 6.2 %copy-start.5 = (f32[2,512,4,128]{1,3,2,0:T(8,128)S(1)}, f32[2,512,4,128]{1,3,2,0:T(8,128)}, u32[]{:S(2)}) copy-start(f32[2,512,4,128]{1,3,2,0:T(8,128)} %get-tuple-element.660) | copy-start | bytes 6291460 | tf_op jit(solution)/shard_map/while
  191.6 3.0 copy-start.3
  201.3 6.2 %copy-start.5 = (f32[2,512,4,128]{1,3,2,0:T(8,128)S(1)}, f32[2,512,4,128]{1,3,2,0:T(8,128)}, u32[]{:S(2)}) copy-start(f32[2,512,4,128]{1,3,2,0:T(8,128)} %get-tuple-element.660) | copy-start | bytes 6291460 | tf_op jit(solution)/shard_map/while
  212.3 3.0 copy-start.3
  222.0 6.2 %copy-start.5 = (f32[2,512,4,128]{1,3,2,0:T(8,128)S(1)}, f32[2,512,4,128]{1,3,2,0:T(8,128)}, u32[]{:S(2)}) copy-start(f32[2,512,4,128]{1,3,2,0:T(8,128)} %get-tuple-element.660) | copy-start | bytes 6291460 | tf_op jit(solution)/shard_map/while
  233.0 3.0 copy-start.3
  242.8 6.2 %copy-start.5 = (f32[2,512,4,128]{1,3,2,0:T(8,128)S(1)}, f32[2,512,4,128]{1,3,2,0:T(8,128)}, u32[]{:S(2)}) copy-start(f32[2,512,4,128]{1,3,2,0:T(8,128)} %get-tuple-element.660) | copy-start | bytes 6291460 | tf_op jit(solution)/shard_map/while
  253.7 3.0 copy-start.3
  260.7 2.8 copy-start.4
  263.5 6.2 %copy-start.5 = (f32[2,512,4,128]{1,3,2,0:T(8,128)S(1)}, f32[2,512,4,128]{1,3,2,0:T(8,128)}, u32[]{:S(2)}) copy-start(f32[2,512,4,128]{1,3,2,0:T(8,128)} %get-tuple-element.660) | copy-start | bytes 6291460 | tf_op jit(solution)/shard_map/while
  274.4 3.0 copy-start.3
  284.2 6.2 %copy-start.5 = (f32[2,512,4,128]{1,3,2,0:T(8,128)S(1)}, f32[2,512,4,128]{1,3,2,0:T(8,128)}, u32[]{:S(2)}) copy-start(f32[2,512,4,128]{1,3,2,0:T(8,128)} %get-tuple-element.660) | copy-start | bytes 6291460 | tf_op jit(solution)/shard_map/while
  295.1 3.0 copy-start.3
  304.9 6.2 %copy-start.5 = (f32[2,512,4,128]{1,3,2,0:T(8,128)S(1)}, f32[2,512,4,128]{1,3,2,0:T(8,128)}, u32[]{:S(2)}) copy-start(f32[2,512,4,128]{1,3,2,0:T(8,128)} %get-tuple-element.660) | copy-start | bytes 6291460 | tf_op jit(solution)/shard_map/while
  315.9 3.0 copy-start.3
  325.6 6.2 %copy-start.5 = (f32[2,512,4,128]{1,3,2,0:T(8,128)S(1)}, f32[2,512,4,128]{1,3,2,0:T(8,128)}, u32[]{:S(2)}) copy-start(f32[2,512,4,128]{1,3,2,0:T(8,128)} %get-tuple-element.660) | copy-start | bytes 6291460 | tf_op jit(solution)/shard_map/while
  340.5 23.7 %all-to-all-start.1 = ((bf16[2,512,512]{2,0,1:T(2,128)(2,1)}), bf16[2,512,512]{2,0,1:T(2,128)(2,1)S(1)}, u32[]{:S(2)}, u32[]{:S(2)}) async-start(bf16[2,512,512]{2,0,1:T(2,128)(2,1)} %copy.67), calls=%async_computation.1 | async-start | bytes 2097152 | tf_op jit(solution)/shard_map/all_to_all | solution.py:124
  365.2 21.6 %all-to-all-start = ((bf16[2,512,512]{2,0,1:T(2,128)(2,1)}), bf16[2,512,512]{2,0,1:T(2,128)(2,1)S(1)}, u32[]{:S(2)}, u32[]{:S(2)}) async-start(bf16[2,512,512]{2,0,1:T(2,128)(2,1)} %copy.66), calls=%async_computation | async-start | bytes 2097152 | tf_op jit(solution)/shard_map/all_to_all | solution.py:125
  (19 other events, 36.0 us)
Sparse Core Ops, SparseCore 0:
  10.2 54.3 all-gather.6
  66.3 51.2 all-gather.10
  119.3 51.5 all-gather.8
where the time goes:
time: 403 us; the launch traced here: 397 us
  waiting for transfers between devices  123 us (31%)
  matrix products  92.1 us (23%)
  other arithmetic  68.2 us (17%)
  blocking collectives  44.8 us (11%)
  local copies, waits for them, and re-layouts  41.7 us (10%)
  between operations  14 us (3%)
  starting transfers between devices  12.5 us (3%)
    all_gather x1, waiting for transfers between devices, on_device(): lax.all_gather(inner_own, 'seq', axis=1, tiled=True)  53.2 us
    reduce_sum x8, other arithmetic, tile(): square = square * factor * factor + jnp.sum(weights * weights, axis=-1)  49.2 us
    all_gather x1, waiting for transfers between devices, on_device(): lax.all_gather(value_own, 'seq', axis=1, tiled=True)  48.3 us
    dot_general x8, matrix products, tile(): jnp.einsum('shqk,skd->sqhd', mixing.astype(jnp.bfloat16), value_blk, pref...  31.7 us
    dot_general x8, matrix products, tile(): jnp.einsum('shqk,skd->sqhd', weights.astype(jnp.bfloat16), value_blk, pre...  27.1 us
    all_gather x1, blocking collectives, on_device(): lax.all_gather(log_decay, 'seq', axis=2, tiled=True)  24.5 us
    dot_general x8, matrix products, tile(): jnp.einsum('sqhd,skd->shqk', query, key_blk, preferred_element_type=jnp.f...  22.1 us
    all_gather x1, blocking collectives, on_device(): lax.all_gather(doc_ids.astype(jnp.float32), 'seq', axis=1, tiled=True)  20.3 us
  transfers between devices with their start and end apart: 5, of which 4 were waited for; matrix products, arithmetic and copies ran while one was open for 7% of the time, Pallas kernels for 0%

commit v1 on v0

v1 whole, which is shorter than its diff:
```python
import math

import jax
import jax.numpy as jnp
from jax import lax
from jax.experimental import pallas as pl
from jax.experimental.pallas import tpu as pltpu
from jax.sharding import PartitionSpec as P

F32, BF16 = jnp.float32, jnp.bfloat16
BLK, HG, SLOTS, TQ = 512, 8, 5, 256
UNROLL = 2
XR = 272
LOG2E = 1.4426950408889634
SC = LOG2E / math.sqrt(128.0)
BIG = 1e30
EPS = 1e-05
NT = (((1,), (1,)), ((), ()))
MESH = pl.DeviceIdType.MESH


def dot_nt(a, b):
    return lax.dot_general(a, b, NT, preferred_element_type=F32)


def dot(a, b):
    return jnp.dot(a, b, preferred_element_type=F32)


def fold_sum(x):
    return jnp.sum(x.reshape(x.shape[0] // 8, 8, x.shape[1]), axis=0)


def fold_max(x):
    return jnp.max(jnp.max(x.reshape(x.shape[0] // 8, 8, x.shape[1]), axis=0), axis=0, keepdims=True)


def prefix_sums(x):
    lane = lax.broadcasted_iota(jnp.int32, x.shape, 1)
    step = 1
    while step < x.shape[1]:
        x = x + jnp.where(lane >= step, pltpu.roll(x, step, 1), 0.0)
        step *= 2
    return x


def to_columns(rows):
    wide = jnp.concatenate([rows, jnp.zeros((120, rows.shape[1]), F32)], axis=0)
    return jnp.transpose(wide)


def t16(x):
    return jnp.transpose(x.astype(F32)).astype(BF16)


class Refs:
    pass


class Place:
    def __init__(self):
        self.s, self.hd = lax.axis_index("seq"), lax.axis_index("head")
        self.z, self.col = self.s // 2, self.s % 2
        self.g, self.c = self.hd // 2, self.hd % 2
        self.sibling = (self.s, self.g * 2 + 1 - self.c)
        self.beside = (self.z * 2 + 1 - self.col, self.hd)
        self.above = (self.s + 2, self.hd)
        self.below = (self.s - 2, self.hd)


def remote(src, dst, send, recv, device):
    return pltpu.make_async_remote_copy(
        src_ref=src, dst_ref=dst, send_sem=send, recv_sem=recv, device_id=device, device_id_type=MESH)


def greet(w):
    barrier = pltpu.get_barrier_semaphore()

    def tell(device):
        pl.semaphore_signal(barrier, inc=1, device_id=device, device_id_type=MESH)

    def others(k, _):
        tell((w.s, (w.hd + k) % 16))
        return 0
    lax.fori_loop(1, 16, others, 0)
    tell(w.beside)

    @pl.when(w.z < 3)
    def _():
        tell(w.above)

    @pl.when(w.z > 0)
    def _():
        tell(w.below)
    pl.semaphore_wait(barrier, 16 + (w.z + 2) // 3 + (5 - w.z) // 3 - 0)


def swap_copies(r, w):
    return (remote(r.query.at[1 - w.c], r.qraw.at[1], r.swap_send.at[0], r.swap_recv.at[0], w.sibling),
            remote(r.aux_in.at[1 - w.c], r.aux_raw.at[1], r.swap_send.at[1], r.swap_recv.at[1], w.sibling))


def part(r, slot, j):
    return r.aux.at[slot] if j == 3 else r.kvb.at[slot, j]


def up_copy(r, w, step, j):
    return remote(part(r, 2 * step, j), part(r, 2 * step + 2, j), r.up_send.at[step, j], r.up_recv.at[step, j], w.above)


def side_copy(r, w, step, j):
    return remote(part(r, 2 * step + 2 * w.col, j), part(r, 2 * step + 1, j), r.side_send.at[step, j], r.side_recv.at[step, j], w.beside)


def sends_up(w, step):
    return (w.z < 3) if step == 0 else ((w.z >= 1) & (w.z < 3))


def sends_side(w, step):
    return w.z >= step + w.col


def gets_up(w, step):
    return w.z >= step + 1


def gets_side(w, step):
    return w.z >= step + 1 - w.col


def load_own(r, w):
    loads = [pltpu.make_async_copy(ref.at[w.c], r.raw.at[i], r.load_sem.at[i])
             for i, ref in enumerate((r.key, r.value, r.inner, r.outer))]
    qload = pltpu.make_async_copy(r.query.at[w.c], r.qraw.at[0], r.load_sem.at[4])
    aload = pltpu.make_async_copy(r.aux_in.at[w.c], r.aux_raw.at[0], r.load_sem.at[5])
    aload.start()
    for x in loads:
        x.start()
    qload.start()
    greet(w)
    swaps = swap_copies(r, w)
    swaps[1].start()
    swaps[0].start()

    def send_part(j):
        @pl.when(sends_up(w, 0))
        def _():
            up_copy(r, w, 0, j).start()

        @pl.when((w.col == 0) & sends_side(w, 0))
        def _():
            side_copy(r, w, 0, j).start()

    aload.wait()
    swaps[1].wait_recv()
    mine, theirs = r.aux_raw[0], r.aux_raw[1]
    first = jnp.where(w.c == 0, mine, theirs)
    second = jnp.where(w.c == 0, theirs, mine)
    r.aux[0, 0:8, :] = jnp.concatenate([first[0:4], second[0:4]], axis=0)
    r.aux[0, 8:16, :] = jnp.broadcast_to(mine[4:5], (8, BLK))
    send_part(3)
    for i in range(4):
        loads[i].wait()
        r.wide[...] = r.raw[i].astype(F32)
        rows = r.wide[pl.ds(w.g, BLK, stride=8), :].astype(BF16)
        if i < 3:
            r.kvb[0, i] = rows
            send_part(i)
        else:
            r.outer_own[...] = rows
    qload.wait()
    swaps[0].wait_recv()
    for i in range(2):
        r.wide[0:2048, :] = r.qraw[i].astype(F32)
        base = 4 * w.c if i == 0 else 4 - 4 * w.c
        for j in range(4):
            r.q[base + j] = r.wide[pl.ds(j, BLK, stride=4), :].astype(BF16)
    for x in swaps:
        x.wait_send()


def take_up(r, w, step):
    for j in (3, 0, 1, 2):
        @pl.when(gets_up(w, step))
        def _():
            up_copy(r, w, step, j).wait_recv()
            if step == 0:
                @pl.when(sends_up(w, 1))
                def _():
                    up_copy(r, w, 1, j).start()

                @pl.when(w.col == 0)
                def _():
                    side_copy(r, w, 1, j).start()

                @pl.when(w.col == 1)
                def _():
                    side_copy(r, w, 0, j).start()
            else:
                @pl.when(w.col == 1)
                def _():
                    side_copy(r, w, 1, j).start()


def take_side(r, w, step):
    @pl.when(gets_side(w, step))
    def _():
        for j in range(4):
            side_copy(r, w, step, j).wait_recv()


def end_sends(r, w):
    for step in range(2):
        @pl.when(sends_up(w, step))
        def _():
            for j in range(4):
                up_copy(r, w, step, j).wait_send()

        @pl.when(sends_side(w, step))
        def _():
            for j in range(4):
                side_copy(r, w, step, j).wait_send()


def own_prepare(r):
    own = prefix_sums(r.aux[0, 0:8, :])
    r.csum[...] = own
    r.csum_col[...] = to_columns(own)
    doc_c = to_columns(r.aux[0, 8:16, :])[:, 0:1]
    cb = dot_nt(r.kvb[0, 2], r.outer_own[...])
    kj = lax.broadcasted_iota(jnp.int32, (BLK, BLK), 0)
    qi = lax.broadcasted_iota(jnp.int32, (BLK, BLK), 1)
    seen = (qi >= kj) & (doc_c == r.aux[0, 8:9, :])
    r.cb[...] = jnp.where(seen, cb, 0.0)
    r.hide[...] = jnp.where(seen, 0.0, -BIG)
    r.xt[0:128, :] = t16(r.kvb[0, 1])
    r.xt[256:XR, :] = jnp.ones((XR - 256, BLK), BF16)
    r.vo[0:128, :] = r.xt[0:128, :]
    r.vo[128:144, :] = jnp.ones((16, BLK), BF16)
    r.tail[...] = jnp.zeros((8, 128), F32)


def own_block(r):
    def head(h, _):
        lanes = lax.broadcasted_iota(jnp.int32, (BLK, 128), 1)
        acol = jnp.sum(jnp.where(lanes == h, r.csum_col[...], 0.0), axis=1, keepdims=True)
        arow = r.csum[pl.ds(h, 1), :]
        for qt in range(BLK // TQ):
            cols = slice(qt * TQ, (qt + 1) * TQ)
            n = (qt + 1) * TQ
            s = dot_nt(r.kvb[0, 0, 0:n, :], r.q[h, cols, :]) + r.hide[0:n, cols]
            m = fold_max(s)
            p = jnp.exp2((s - m) * SC)
            mix = jnp.exp2(jnp.minimum((arow[:, cols] - acol[0:n]) * LOG2E, 0.0)) * r.cb[0:n, cols]
            av = dot(r.vo[:, 0:n], p.astype(BF16))
            r.m[h, :, cols] = jnp.broadcast_to(m, (8, TQ))
            r.sq[h, :, cols] = fold_sum(p * p)
            r.cross[h, :, cols] = fold_sum(p * mix)
            r.mixsq[h, :, cols] = fold_sum(mix * mix)
            r.acc[h, 0:128, cols] = av[0:128]
            r.acc[h, 128:256, cols] = jnp.zeros((128, TQ), F32)
            r.acc[h, 256:XR, cols] = av[128:144]
            r.stud[h, :, cols] = dot(r.vo[0:128, 0:n], mix.astype(BF16))
        r.state[h] = jnp.zeros((256, 128), F32)
        return 0
    lax.fori_loop(0, HG, head, 0)


def prev_block(r, slot):
    sums = prefix_sums(r.aux[slot, 0:8, :])
    whole = sums[:, BLK - 1:BLK]
    doc_last = r.aux[1, 8:9, BLK - 1:BLK]
    weight = jnp.exp(whole - sums + r.tail[:, 0:1])
    r.tail[...] = r.tail[...] + whole
    r.bdec[...] = jnp.where(r.aux[slot, 8:9, :] == doc_last, weight, 0.0)
    doc_c = to_columns(r.aux[slot, 8:16, :])[:, 0:1]
    r.kmask[...] = jnp.broadcast_to(jnp.where(doc_c == doc_last, 0.0, -BIG), (BLK, 128))
    r.qoff[...] = jnp.broadcast_to(jnp.where(r.aux[0, 8:9, :] == doc_last, 0.0, -BIG), (8, BLK))
    r.xt[0:128, :] = t16(r.kvb[slot, 1])
    r.bt[...] = jnp.transpose(r.kvb[slot, 2].astype(F32))

    def score(h, qt):
        cols = slice(qt * TQ, (qt + 1) * TQ)
        return dot_nt(r.kvb[slot, 0], r.q[h, cols, :])

    def soft(h, qt, s):
        cols = slice(qt * TQ, (qt + 1) * TQ)
        km = r.kmask[...]
        s = s + jnp.concatenate([km] * (TQ // 128), axis=1)
        qoff = r.qoff[0:1, cols]
        m_old = r.m[h, 0:1, cols]
        m = jnp.maximum(m_old, fold_max(s) + qoff)
        f = jnp.exp2((m_old - m) * SC)
        p = jnp.exp2((s - (m - qoff)) * SC)
        r.m[h, :, cols] = jnp.broadcast_to(m, (8, TQ))
        r.sq[h, :, cols] = r.sq[h, :, cols] * (f * f) + fold_sum(p * p)
        r.cross[h, :, cols] = r.cross[h, :, cols] * f
        return p.astype(BF16), f

    def apply(h, qt, xt, p, f):
        cols = slice(qt * TQ, (qt + 1) * TQ)
        r.acc[h, :, cols] = r.acc[h, :, cols] * f + dot(xt, p)

    def heads(i, _):
        units = [(i * UNROLL + u, qt) for u in range(UNROLL) for qt in range(BLK // TQ)]
        xts = []
        for u in range(UNROLL):
            h = i * UNROLL + u
            xb = (r.bt[...] * r.bdec[pl.ds(h, 1), :]).astype(BF16)
            xts.append(jnp.concatenate([r.xt[0:128, :], xb, r.xt[256:XR, :]], axis=0))
            r.state[h] = r.state[h] + dot_nt(xts[u][0:256], xb)
        nxt = score(*units[0])
        prev = None
        for j, (h, qt) in enumerate(units):
            cur = nxt
            if j + 1 < len(units):
                nxt = score(*units[j + 1])
            pf = soft(h, qt, cur)
            if prev is not None:
                apply(*prev)
            prev = (h, qt, xts[j // (BLK // TQ)]) + pf
        apply(*prev)
        return 0
    lax.fori_loop(0, HG // UNROLL, heads, 0)


def finish(r, w):
    doc_last = r.aux[1, 8:9, BLK - 1:BLK]
    from_prev = jnp.where((r.aux[0, 8:9, :] == doc_last) & (w.s > 0), 1.0, 0.0)
    r.ct[...] = jnp.transpose(r.outer_own[...].astype(F32))
    r.ssq[...] = jnp.zeros((8, BLK), F32)

    def head(h, _):
        cf = r.ct[...]
        a = jnp.exp(r.csum[pl.ds(h, 1), :]) * from_prev
        y = dot_nt(r.state[h].astype(BF16), r.outer_own[...])
        inv = 1.0 / r.acc[h, 256:257, :]
        tf = r.acc[h, 0:128, :] * inv
        sf = r.stud[h] + a * y[0:128, :]
        r.teach[h] = jnp.transpose(tf).astype(BF16)
        r.student[h] = jnp.transpose(sf).astype(BF16)
        terms = (r.mixsq[h] + (a * a) * fold_sum(y[128:256, :] * cf)
                 - (2.0 * inv) * (r.cross[h] + a * fold_sum(cf * r.acc[h, 128:256, :]))
                 + (inv * inv) * r.sq[h])
        r.err[pl.ds(h, 1), :] = jnp.sum(terms, axis=0, keepdims=True)
        r.ssq[0:1, :] = r.ssq[0:1, :] + jnp.sum(fold_sum(tf * tf), axis=0, keepdims=True)
        r.ssq[1:2, :] = r.ssq[1:2, :] + jnp.sum(fold_sum(sf * sf), axis=0, keepdims=True)
        return 0
    lax.fori_loop(0, HG, head, 0)


def ssq_copy(r, w, k):
    return remote(r.ssq, r.ssq_all.at[w.g], r.ssq_send.at[k], r.ssq_recv.at[w.g], (w.s, ((w.g + k) % 8) * 2 + w.c))


def ssq_from(r, w, k):
    g = (w.g + 8 - k) % 8
    return remote(r.ssq, r.ssq_all.at[g], r.ssq_send.at[k], r.ssq_recv.at[g], (w.s, g * 2 + w.c))


def out_copy(r, w, k):
    to = (w.hd + k) % 16
    return remote(r.gap.at[pl.ds(pl.multiple_of(to * 32, 32), 32)],
                  r.out.at[w.c, :, pl.ds(pl.multiple_of(w.g * 1024, 1024), 1024)],
                  r.out_send.at[k], r.out_recv.at[w.hd], (w.s, to))


def out_from(r, w, k):
    sender = (w.hd + 16 - k) % 16
    return remote(r.gap.at[0:32],
                  r.out.at[sender % 2, :, pl.ds(pl.multiple_of((sender // 2) * 1024, 1024), 1024)],
                  r.out_send.at[k], r.out_recv.at[sender], (w.s, sender))


def share(r, w):
    for k in range(1, 8):
        ssq_copy(r, w, k).start()
    r.ssq_all[pl.ds(w.g, 1)] = r.ssq[...].reshape(1, 8, BLK)
    top, bottom = r.err[0:4, :], r.err[4:8, :]
    filler = jnp.zeros((4, BLK), F32)
    r.err_pair[0] = jnp.concatenate([jnp.where(w.c == 0, top, bottom), filler], axis=0)
    r.err_pair[1] = jnp.concatenate([jnp.where(w.c == 0, bottom, top), filler], axis=0)
    err_far = remote(r.err_pair.at[1], r.err_out.at[w.c], r.swap_send.at[2], r.swap_recv.at[2], w.sibling)
    err_far.start()
    err_near = pltpu.make_async_copy(r.err_pair.at[0], r.err_out.at[w.c], r.load_sem.at[0])
    err_near.start()
    for k in range(1, 8):
        ssq_from(r, w, k).wait_recv()
    sums = jnp.sum(r.ssq_all[...], axis=0)
    scale = lax.rsqrt(sums / (8.0 * HG * 128) + EPS)
    cols = to_columns(scale)
    t_scale, s_scale = cols[:, 0:1], cols[:, 1:2]
    gain = r.gain[pl.ds(w.g, 1), :]
    for h in range(HG):
        lanes = slice(h * 128, (h + 1) * 128)
        gap = gain[:, lanes] * r.student[h].astype(F32) * s_scale - r.teach[h].astype(F32) * t_scale
        r.gap[:, lanes] = gap.astype(BF16)
    for k in range(1, 16):
        out_copy(r, w, k).start()
    own = pltpu.make_async_copy(
        r.gap.at[pl.ds(pl.multiple_of(w.hd * 32, 32), 32)],
        r.out.at[w.c, :, pl.ds(pl.multiple_of(w.g * 1024, 1024), 1024)], r.load_sem.at[1])
    own.start()
    err_near.wait()
    own.wait()
    err_far.wait_send()
    remote(r.err_pair.at[1], r.err_out.at[1 - w.c], r.swap_send.at[2], r.swap_recv.at[2], w.sibling).wait_recv()
    for k in range(1, 16):
        out_from(r, w, k).wait_recv()
    for k in range(1, 8):
        ssq_copy(r, w, k).wait_send()
    for k in range(1, 16):
        out_copy(r, w, k).wait_send()


ARGS = ("query", "key", "value", "inner", "outer", "aux_in", "gain")
OUTS = ("out", "err_out")
DMA = pltpu.SemaphoreType.DMA
SCRATCH = dict(
    qraw=pltpu.VMEM((2, 2048, 128), BF16), aux_raw=pltpu.VMEM((2, 8, BLK), F32),
    raw=pltpu.VMEM((4, 4096, 128), BF16), wide=pltpu.VMEM((4096, 128), F32),
    q=pltpu.VMEM((HG, BLK, 128), BF16), kvb=pltpu.VMEM((SLOTS, 3, BLK, 128), BF16),
    aux=pltpu.VMEM((SLOTS, 16, BLK), F32), outer_own=pltpu.VMEM((BLK, 128), BF16),
    csum=pltpu.VMEM((8, BLK), F32), csum_col=pltpu.VMEM((BLK, 128), F32),
    cb=pltpu.VMEM((BLK, BLK), F32), hide=pltpu.VMEM((BLK, BLK), F32),
    m=pltpu.VMEM((HG, 8, BLK), F32), sq=pltpu.VMEM((HG, 8, BLK), F32),
    cross=pltpu.VMEM((HG, 8, BLK), F32), mixsq=pltpu.VMEM((HG, 8, BLK), F32),
    acc=pltpu.VMEM((HG, XR, BLK), F32), stud=pltpu.VMEM((HG, 128, BLK), F32),
    state=pltpu.VMEM((HG, 256, 128), F32), bdec=pltpu.VMEM((8, BLK), F32), tail=pltpu.VMEM((8, 128), F32),
    kmask=pltpu.VMEM((BLK, 128), F32), qoff=pltpu.VMEM((8, BLK), F32),
    xt=pltpu.VMEM((XR, BLK), BF16), vo=pltpu.VMEM((144, BLK), BF16), bt=pltpu.VMEM((128, BLK), F32),
    ct=pltpu.VMEM((128, BLK), F32),
    teach=pltpu.VMEM((HG, BLK, 128), BF16), student=pltpu.VMEM((HG, BLK, 128), BF16),
    err=pltpu.VMEM((8, BLK), F32), err_pair=pltpu.VMEM((2, 8, BLK), F32),
    ssq=pltpu.VMEM((8, BLK), F32), ssq_all=pltpu.VMEM((8, 8, BLK), F32), gap=pltpu.VMEM((BLK, HG * 128), BF16),
    load_sem=DMA((6,)), swap_send=DMA((3,)), swap_recv=DMA((3,)),
    up_send=DMA((2, 4)), up_recv=DMA((2, 4)), side_send=DMA((2, 4)), side_recv=DMA((2, 4)),
    ssq_send=DMA((8,)), ssq_recv=DMA((8,)), out_send=DMA((16,)), out_recv=DMA((16,)),
)


def kernel(*refs):
    r = Refs()
    for name, ref in zip(ARGS + OUTS + tuple(SCRATCH), refs):
        setattr(r, name, ref)
    w = Place()
    load_own(r, w)
    own_prepare(r)
    own_block(r)

    @pl.when(w.s == 0)
    def _():
        r.aux[1] = jnp.zeros((16, BLK), F32)
    take_up(r, w, 0)
    take_side(r, w, 0)

    def earlier(slot, _):
        prev_block(r, slot)
        return 0
    lax.fori_loop(1, jnp.minimum(w.s, 2) + 1, earlier, 0)
    take_up(r, w, 1)
    take_side(r, w, 1)
    lax.fori_loop(3, jnp.minimum(w.s, 4) + 1, earlier, 0)
    finish(r, w)
    share(r, w)
    end_sends(r, w)


def on_device(query_rows, key_rows, value_rows, state_in, state_out, log_decay, doc_ids, norm_gain):
    docs = jnp.broadcast_to(doc_ids.astype(F32)[:, None, :], (2, 4, BLK))
    aux_in = jnp.concatenate([log_decay, docs], axis=1)
    flat = [x.reshape(2, -1, 128) for x in (query_rows, key_rows, value_rows, state_in, state_out)]
    out, err = pl.pallas_call(
        kernel,
        out_shape=(jax.ShapeDtypeStruct((2, 32, 8192), BF16), jax.ShapeDtypeStruct((2, 8, BLK), F32)),
        in_specs=[pl.BlockSpec(memory_space=pl.ANY)] * 6 + [pl.BlockSpec(memory_space=pltpu.VMEM)],
        out_specs=(pl.BlockSpec(memory_space=pl.ANY), pl.BlockSpec(memory_space=pl.ANY)),
        scratch_shapes=list(SCRATCH.values()),
        compiler_params=pltpu.CompilerParams(collective_id=0, has_side_effects=True, vmem_limit_bytes=56 * 2**20),
        cost_estimate=pl.CostEstimate(flops=10**10, bytes_accessed=10**7, transcendentals=0),
    )(*flat, aux_in, norm_gain.reshape(8, 1024))
    return (out, err[:, 0:4, :])


def solution(mesh):
    placed = (
        P(None, "seq", "head", None),
        P(None, "seq", None, None),
        P(None, "seq", None, None),
        P(None, "seq", None, None),
        P(None, "seq", None, None),
        P(None, "head", "seq"),
        P(None, "seq"),
        P(),
    )
    return jax.shard_map(
        on_device,
        mesh=mesh,
        in_specs=placed,
        out_specs=(P(None, ("seq", "head"), None), P(None, "head", "seq")),
        check_vma=False,
    )
```

time: 403 us -> 85.9 us (0.21); the launches traced: 397 us -> 85.4 us
  waiting for transfers between devices: 123 us -> 0 us
  matrix products: 92.1 us -> 0 us
  Pallas kernels: 0 us -> 77.7 us
  other arithmetic: 68.2 us -> 2.03 us
  blocking collectives: 44.8 us -> 0 us
  local copies, waits for them, and re-layouts: 41.7 us -> 5.02 us
  between operations: 14 us -> 0.64 us
  starting transfers between devices: 12.5 us -> 0 us
    all_gather x3 -> x0, waiting for transfers between devices: 102 us -> none  [the longest x1 53.2 us: on_device(): lax.all_gather(inner_own, 'seq', axis=1, tiled=True)]
    dot_general x32 -> x0, matrix products: 92.1 us -> none  [the longest x8 31.7 us: tile(): jnp.einsum('shqk,skd->sqhd', mixing.astype(jnp.bfloat16), value_blk, pref...]
    pallas_call x0 -> x1, Pallas kernels: none -> 77.7 us  [on_device(): pl.pallas_call(kernel, out_shape=(jax.ShapeDtypeStruct((2, 32, 8192), BF1...]
    reduce_sum x12 -> x0, other arithmetic: 51 us -> none  [the longest x8 49.2 us: tile(): square = square * factor * factor + jnp.sum(weights * weights, axis=-1)]
    all_gather x2 -> x0, blocking collectives: 44.8 us -> none  [the longest x1 24.5 us: on_device(): lax.all_gather(log_decay, 'seq', axis=2, tiled=True)]
    all_to_all x2 -> x0, waiting for transfers between devices: 21.2 us -> none  [the longest x1 11.1 us: on_device(): lax.all_to_all(stud_rows, 'head', split_axis=1, concat_axis=2, tiled=True)]
    dynamic_slice x21 -> x0, local copies, waits for them, and re-layouts: 14.7 us -> none  [the longest x8 6.96 us: tile(): cum_key = lax.dynamic_slice_in_dim(cum_all, kstart, width, 2)]
    all_to_all x2 -> x0, starting transfers between devices: 12.4 us -> none  [the longest x1 7.23 us: on_device(): lax.all_to_all(teach_rows, 'head', split_axis=1, concat_axis=2, tiled=True)]
  transfers between devices with their start and end apart: 5 -> 0, of which waited for: 4 -> 0; matrix products, arithmetic and copies ran while one was open for 7% -> 0% of each run, Pallas kernels for 0% -> 0%
where the time goes in v1:
time: 85.9 us; the launch traced here: 85.4 us
  Pallas kernels  77.7 us (90%)
  local copies, waits for them, and re-layouts  5.02 us (6%)
  other arithmetic  2.03 us (2%)
    pallas_call x1, Pallas kernels, on_device(): pl.pallas_call(kernel, out_shape=(jax.ShapeDtypeStruct((2, 32, 8192), BF1...  77.7 us
    unnamed x1, local copies, waits for them, and re-layouts  2.26 us

profile of v1, /device:TPU:89, one launch (start us, length us, event | category | flops | bytes accessed | tf_op | source)
XLA Modules:
  0.0 85.4 jit_solution(5367040342222632722)
XLA Ops:
  0.6 0.7 convert_element_type.3
  1.3 1.3 %pad_maximum_fusion.refs_5_ = f32[2,8,512]{2,1,0:T(8,128)} fusion(f32[2,4,512]{2,1,0:T(4,128)S(1)} %broadcast_in_dim.2, f32[2,4,512]{2,1,0:T(4,128)} %param.13), kind=kLoop, calls=%fused_computation | loop fusion | flops 8192 | bytes 65536 | tf_op jit(solution)/shard_map/concatenate | solution.py:471
  2.7 1.4 %reshape.28.refs_6_ = f32[8,1024]{1,0:T(8,128)} reshape(f32[8192]{0:T(1024)} %param.15) | data formatting | bytes 65536 | tf_op jit(solution)/shard_map/reshape | solution.py:481
  4.1 77.7 %shard_map.95 = (bf16[2,32,8192]{2,1,0:T(8,128)(2,1)}, f32[2,8,512]{2,1,0:T(8,128)}) custom-call(bf16[2,2048,128]{2,1,0:T(8,128)(2,1)} %bitcast.9, bf16[2,4096,128]{2,1,0:T(8,128)(2,1)} %bitcast.5, bf16[2,4096,128]{2,1,0:T(8,128)(2,1)} %bitcast.6, bf16[2,4096,128]{2,1,0:T(8,128)(2,1)} %bitcast.7, bf16[2,4096,128]{2,1,0:T(8,128)(2,1)} %bitcast.8, ...), custom_call_target="tpu_custom_call" | custom-call | flops 10000000000 | bytes 10000000 | tf_op jit(solution)/shard_map/pallas_call | solution.py:473
  81.8 1.4 %slice.3 = f32[2,4,512]{2,1,0:T(4,128)} slice(f32[2,8,512]{2,1,0:T(8,128)} %get-tuple-element.5), slice={[0:2], [0:4], [0:512]} | slice | bytes 32768 | tf_op jit(solution)/shard_map/slice | solution.py:482
  83.2 2.3 %copy.11 = bf16[2,32,8192]{2,1,0:T(8,128)(2,1)} copy(bf16[2,32,8192]{2,1,0:T(8,128)(2,1)} %get-tuple-element.8) | data formatting | bytes 2097152
  (1 shorter events, 0.0 us)

commit v2 on v1

--- a/solution.py
+++ b/solution.py
@@ -97,7 +97,7 @@
 
 def swap_copies(r, w):
     return (remote(r.query.at[1 - w.c], r.qraw.at[1], r.swap_send.at[0], r.swap_recv.at[0], w.sibling),
-            remote(r.aux_in.at[1 - w.c], r.aux_raw.at[1], r.swap_send.at[1], r.swap_recv.at[1], w.sibling))
+            remote(r.decay.at[1 - w.c], r.decay_raw.at[1], r.swap_send.at[1], r.swap_recv.at[1], w.sibling))
 
 
 def part(r, slot, j):
@@ -132,7 +132,7 @@
     loads = [pltpu.make_async_copy(ref.at[w.c], r.raw.at[i], r.load_sem.at[i])
              for i, ref in enumerate((r.key, r.value, r.inner, r.outer))]
     qload = pltpu.make_async_copy(r.query.at[w.c], r.qraw.at[0], r.load_sem.at[4])
-    aload = pltpu.make_async_copy(r.aux_in.at[w.c], r.aux_raw.at[0], r.load_sem.at[5])
+    aload = pltpu.make_async_copy(r.decay.at[w.c], r.decay_raw.at[0], r.load_sem.at[5])
     aload.start()
     for x in loads:
         x.start()
@@ -153,11 +153,12 @@
 
     aload.wait()
     swaps[1].wait_recv()
-    mine, theirs = r.aux_raw[0], r.aux_raw[1]
+    mine, theirs = r.decay_raw[0], r.decay_raw[1]
     first = jnp.where(w.c == 0, mine, theirs)
     second = jnp.where(w.c == 0, theirs, mine)
-    r.aux[0, 0:8, :] = jnp.concatenate([first[0:4], second[0:4]], axis=0)
-    r.aux[0, 8:16, :] = jnp.broadcast_to(mine[4:5], (8, BLK))
+    r.aux[0, 0:8, :] = jnp.concatenate([first, second], axis=0)
+    docs = jnp.where(w.c == 0, r.docs[0:1, :], r.docs[1:2, :]).astype(F32)
+    r.aux[0, 8:16, :] = jnp.broadcast_to(docs, (8, BLK))
     send_part(3)
     for i in range(4):
         loads[i].wait()
@@ -179,34 +180,26 @@
         x.wait_send()
 
 
-def take_up(r, w, step):
-    for j in (3, 0, 1, 2):
-        @pl.when(gets_up(w, step))
-        def _():
+def take_up(r, w, step, parts):
+    @pl.when(gets_up(w, step))
+    def _():
+        for j in parts:
             up_copy(r, w, step, j).wait_recv()
             if step == 0:
                 @pl.when(sends_up(w, 1))
                 def _():
                     up_copy(r, w, 1, j).start()
 
-                @pl.when(w.col == 0)
-                def _():
-                    side_copy(r, w, 1, j).start()
-
-                @pl.when(w.col == 1)
-                def _():
-                    side_copy(r, w, 0, j).start()
+                side_copy(r, w, 1 - w.col, j).start()
             else:
                 @pl.when(w.col == 1)
                 def _():
                     side_copy(r, w, 1, j).start()
 
 
-def take_side(r, w, step):
-    @pl.when(gets_side(w, step))
-    def _():
-        for j in range(4):
-            side_copy(r, w, step, j).wait_recv()
+def take_side(r, w, step, parts):
+    for j in parts:
+        side_copy(r, w, step, j).wait_recv()
 
 
 def end_sends(r, w):
@@ -237,10 +230,9 @@
     r.xt[256:XR, :] = jnp.ones((XR - 256, BLK), BF16)
     r.vo[0:128, :] = r.xt[0:128, :]
     r.vo[128:144, :] = jnp.ones((16, BLK), BF16)
-    r.tail[...] = jnp.zeros((8, 128), F32)
-
-
-def own_block(r):
+
+
+def own_block(r, start, stop):
     def head(h, _):
         lanes = lax.broadcasted_iota(jnp.int32, (BLK, 128), 1)
         acol = jnp.sum(jnp.where(lanes == h, r.csum_col[...], 0.0), axis=1, keepdims=True)
@@ -263,15 +255,17 @@
             r.stud[h, :, cols] = dot(r.vo[0:128, 0:n], mix.astype(BF16))
         r.state[h] = jnp.zeros((256, 128), F32)
         return 0
-    lax.fori_loop(0, HG, head, 0)
-
-
-def prev_block(r, slot):
+    lax.fori_loop(start, stop, head, 0)
+
+
+def prev_block(r, w, slot, between=None):
     sums = prefix_sums(r.aux[slot, 0:8, :])
     whole = sums[:, BLK - 1:BLK]
     doc_last = r.aux[1, 8:9, BLK - 1:BLK]
-    weight = jnp.exp(whole - sums + r.tail[:, 0:1])
-    r.tail[...] = r.tail[...] + whole
+    tail = jnp.zeros((8, 1), F32)
+    for t in range(1, slot):
+        tail = tail + jnp.sum(r.aux[t, 0:8, :], axis=1, keepdims=True)
+    weight = jnp.exp(whole - sums + tail)
     r.bdec[...] = jnp.where(r.aux[slot, 8:9, :] == doc_last, weight, 0.0)
     doc_c = to_columns(r.aux[slot, 8:16, :])[:, 0:1]
     r.kmask[...] = jnp.broadcast_to(jnp.where(doc_c == doc_last, 0.0, -BIG), (BLK, 128))
@@ -321,7 +315,11 @@
             prev = (h, qt, xts[j // (BLK // TQ)]) + pf
         apply(*prev)
         return 0
-    lax.fori_loop(0, HG // UNROLL, heads, 0)
+    half = HG // UNROLL // 2
+    lax.fori_loop(0, half, heads, 0)
+    if between is not None:
+        between()
+    lax.fori_loop(half, 2 * half, heads, 0)
 
 
 def finish(r, w):
@@ -377,9 +375,8 @@
         ssq_copy(r, w, k).start()
     r.ssq_all[pl.ds(w.g, 1)] = r.ssq[...].reshape(1, 8, BLK)
     top, bottom = r.err[0:4, :], r.err[4:8, :]
-    filler = jnp.zeros((4, BLK), F32)
-    r.err_pair[0] = jnp.concatenate([jnp.where(w.c == 0, top, bottom), filler], axis=0)
-    r.err_pair[1] = jnp.concatenate([jnp.where(w.c == 0, bottom, top), filler], axis=0)
+    r.err_pair[0] = jnp.where(w.c == 0, top, bottom)
+    r.err_pair[1] = jnp.where(w.c == 0, bottom, top)
     err_far = remote(r.err_pair.at[1], r.err_out.at[w.c], r.swap_send.at[2], r.swap_recv.at[2], w.sibling)
     err_far.start()
     err_near = pltpu.make_async_copy(r.err_pair.at[0], r.err_out.at[w.c], r.load_sem.at[0])
@@ -390,7 +387,7 @@
     scale = lax.rsqrt(sums / (8.0 * HG * 128) + EPS)
     cols = to_columns(scale)
     t_scale, s_scale = cols[:, 0:1], cols[:, 1:2]
-    gain = r.gain[pl.ds(w.g, 1), :]
+    gain = r.gain[pl.ds(pl.multiple_of(w.g * 1024, 1024), 1024)].reshape(1, 1024)
     for h in range(HG):
         lanes = slice(h * 128, (h + 1) * 128)
         gap = gain[:, lanes] * r.student[h].astype(F32) * s_scale - r.teach[h].astype(F32) * t_scale
@@ -413,11 +410,11 @@
         out_copy(r, w, k).wait_send()
 
 
-ARGS = ("query", "key", "value", "inner", "outer", "aux_in", "gain")
+ARGS = ("query", "key", "value", "inner", "outer", "decay", "docs", "gain")
 OUTS = ("out", "err_out")
 DMA = pltpu.SemaphoreType.DMA
 SCRATCH = dict(
-    qraw=pltpu.VMEM((2, 2048, 128), BF16), aux_raw=pltpu.VMEM((2, 8, BLK), F32),
+    qraw=pltpu.VMEM((2, 2048, 128), BF16), decay_raw=pltpu.VMEM((2, 4, BLK), F32),
     raw=pltpu.VMEM((4, 4096, 128), BF16), wide=pltpu.VMEM((4096, 128), F32),
     q=pltpu.VMEM((HG, BLK, 128), BF16), kvb=pltpu.VMEM((SLOTS, 3, BLK, 128), BF16),
     aux=pltpu.VMEM((SLOTS, 16, BLK), F32), outer_own=pltpu.VMEM((BLK, 128), BF16),
@@ -426,12 +423,12 @@
     m=pltpu.VMEM((HG, 8, BLK), F32), sq=pltpu.VMEM((HG, 8, BLK), F32),
     cross=pltpu.VMEM((HG, 8, BLK), F32), mixsq=pltpu.VMEM((HG, 8, BLK), F32),
     acc=pltpu.VMEM((HG, XR, BLK), F32), stud=pltpu.VMEM((HG, 128, BLK), F32),
-    state=pltpu.VMEM((HG, 256, 128), F32), bdec=pltpu.VMEM((8, BLK), F32), tail=pltpu.VMEM((8, 128), F32),
+    state=pltpu.VMEM((HG, 256, 128), F32), bdec=pltpu.VMEM((8, BLK), F32),
     kmask=pltpu.VMEM((BLK, 128), F32), qoff=pltpu.VMEM((8, BLK), F32),
     xt=pltpu.VMEM((XR, BLK), BF16), vo=pltpu.VMEM((144, BLK), BF16), bt=pltpu.VMEM((128, BLK), F32),
     ct=pltpu.VMEM((128, BLK), F32),
     teach=pltpu.VMEM((HG, BLK, 128), BF16), student=pltpu.VMEM((HG, BLK, 128), BF16),
-    err=pltpu.VMEM((8, BLK), F32), err_pair=pltpu.VMEM((2, 8, BLK), F32),
+    err=pltpu.VMEM((8, BLK), F32), err_pair=pltpu.VMEM((2, 4, BLK), F32),
     ssq=pltpu.VMEM((8, BLK), F32), ssq_all=pltpu.VMEM((8, 8, BLK), F32), gap=pltpu.VMEM((BLK, HG * 128), BF16),
     load_sem=DMA((6,)), swap_send=DMA((3,)), swap_recv=DMA((3,)),
     up_send=DMA((2, 4)), up_recv=DMA((2, 4)), side_send=DMA((2, 4)), side_recv=DMA((2, 4)),
@@ -446,40 +443,58 @@
     w = Place()
     load_own(r, w)
     own_prepare(r)
-    own_block(r)
+    own_block(r, 0, 4)
+    take_up(r, w, 0, (3, 0))
+    own_block(r, 4, 8)
+    take_up(r, w, 0, (1, 2))
 
     @pl.when(w.s == 0)
     def _():
         r.aux[1] = jnp.zeros((16, BLK), F32)
-    take_up(r, w, 0)
-    take_side(r, w, 0)
-
-    def earlier(slot, _):
-        prev_block(r, slot)
-        return 0
-    lax.fori_loop(1, jnp.minimum(w.s, 2) + 1, earlier, 0)
-    take_up(r, w, 1)
-    take_side(r, w, 1)
-    lax.fori_loop(3, jnp.minimum(w.s, 4) + 1, earlier, 0)
+
+    @pl.when(gets_side(w, 0))
+    def _():
+        side_copy(r, w, 0, 3).wait_recv()
+
+    @pl.when(w.s >= 2)
+    def _():
+        prev_block(r, w, 2, lambda: take_up(r, w, 1, (3, 0)))
+        take_up(r, w, 1, (1, 2))
+
+    @pl.when(w.s >= 1)
+    def _():
+        take_side(r, w, 0, (0, 1, 2))
+        prev_block(r, w, 1)
+
+    @pl.when(w.s >= 4)
+    def _():
+        take_side(r, w, 1, (3,))
+        prev_block(r, w, 4)
+
+    @pl.when(w.s == 3)
+    def _():
+        take_side(r, w, 1, (3,))
+
+    @pl.when(w.s >= 3)
+    def _():
+        take_side(r, w, 1, (0, 1, 2))
+        prev_block(r, w, 3)
     finish(r, w)
     share(r, w)
     end_sends(r, w)
 
 
 def on_device(query_rows, key_rows, value_rows, state_in, state_out, log_decay, doc_ids, norm_gain):
-    docs = jnp.broadcast_to(doc_ids.astype(F32)[:, None, :], (2, 4, BLK))
-    aux_in = jnp.concatenate([log_decay, docs], axis=1)
     flat = [x.reshape(2, -1, 128) for x in (query_rows, key_rows, value_rows, state_in, state_out)]
-    out, err = pl.pallas_call(
+    return pl.pallas_call(
         kernel,
-        out_shape=(jax.ShapeDtypeStruct((2, 32, 8192), BF16), jax.ShapeDtypeStruct((2, 8, BLK), F32)),
-        in_specs=[pl.BlockSpec(memory_space=pl.ANY)] * 6 + [pl.BlockSpec(memory_space=pltpu.VMEM)],
+        out_shape=(jax.ShapeDtypeStruct((2, 32, 8192), BF16), jax.ShapeDtypeStruct((2, 4, BLK), F32)),
+        in_specs=[pl.BlockSpec(memory_space=pl.ANY)] * 6 + [pl.BlockSpec(memory_space=pltpu.VMEM)] * 2,
         out_specs=(pl.BlockSpec(memory_space=pl.ANY), pl.BlockSpec(memory_space=pl.ANY)),
         scratch_shapes=list(SCRATCH.values()),
         compiler_params=pltpu.CompilerParams(collective_id=0, has_side_effects=True, vmem_limit_bytes=56 * 2**20),
         cost_estimate=pl.CostEstimate(flops=10**10, bytes_accessed=10**7, transcendentals=0),
-    )(*flat, aux_in, norm_gain.reshape(8, 1024))
-    return (out, err[:, 0:4, :])
+    )(*flat, log_decay, doc_ids, norm_gain)
 
 
 def solution(mesh):

time: 85.9 us -> 74.2 us (0.86)
  Pallas kernels: 77.7 us -> 70 us
  local copies, waits for them, and re-layouts: 5.02 us -> 2.88 us
  other arithmetic: 2.03 us -> 0 us
    pallas_call x1, Pallas kernels: 77.7 us -> 70 us  [on_device(): pl.pallas_call(kernel, out_shape=(jax.ShapeDtypeStruct((2, 32, 8192), BF1...]
    reshape x1 -> x0, local copies, waits for them, and re-layouts: 1.38 us -> none  [on_device(): norm_gain.reshape(8, 1024)]
    slice x1 -> x0, local copies, waits for them, and re-layouts: 1.37 us -> none  [on_device(): return (out, err[:, 0:4, :])]
    concatenate x1 -> x0, other arithmetic: 1.34 us -> none  [on_device(): aux_in = jnp.concatenate([log_decay, docs], axis=1)]
    unnamed x1 -> x4, local copies, waits for them, and re-layouts: 2.26 us -> 2.88 us
where the time goes in v2:
time: 74.2 us; the launch traced here: 73.5 us
  Pallas kernels  70 us (94%)
  local copies, waits for them, and re-layouts  2.88 us (4%)
    pallas_call x1, Pallas kernels, on_device(): pl.pallas_call(kernel, out_shape=(jax.ShapeDtypeStruct((2, 32, 8192), BF1...  70 us
    unnamed x4, local copies, waits for them, and re-layouts  2.88 us

profile of v2, /device:TPU:89, one launch (start us, length us, event | category | flops | bytes accessed | tf_op | source)
XLA Modules:
  0.0 73.5 jit_solution(10899945051789031285)
XLA Ops:
  0.6 70.0 %shard_map.95 = (bf16[2,32,8192]{2,1,0:T(8,128)(2,1)}, f32[2,4,512]{2,1,0:T(4,128)}) custom-call(bf16[2,2048,128]{2,1,0:T(8,128)(2,1)} %bitcast.9, bf16[2,4096,128]{2,1,0:T(8,128)(2,1)} %bitcast.5, bf16[2,4096,128]{2,1,0:T(8,128)(2,1)} %bitcast.6, bf16[2,4096,128]{2,1,0:T(8,128)(2,1)} %bitcast.7, bf16[2,4096,128]{2,1,0:T(8,128)(2,1)} %bitcast.8, ...), custom_call_target="tpu_custom_call" | custom-call | flops 10000000000 | bytes 10000000 | tf_op jit(solution)/shard_map/pallas_call | solution.py:489
  70.6 0.0 copy-start
  70.7 2.3 %copy.12 = bf16[2,32,8192]{2,1,0:T(8,128)(2,1)} copy(bf16[2,32,8192]{2,1,0:T(8,128)(2,1)} %get-tuple-element.4) | data formatting | bytes 2097152
  72.9 0.0 copy-done
  72.9 0.6 copy.13
Async XLA Ops:
  70.6 2.3 %copy-start = (f32[2,4,512]{2,1,0:T(4,128)S(1)}, f32[2,4,512]{2,1,0:T(4,128)}, u32[]{:S(2)}) copy-start(f32[2,4,512]{2,1,0:T(4,128)} %get-tuple-element.5) | copy-start | bytes 49156

commit v3 on v2

v3 whole, which is shorter than its diff:
```python
import math

import jax
import jax.numpy as jnp
from jax import lax
from jax.experimental import pallas as pl
from jax.experimental.pallas import tpu as pltpu
from jax.sharding import PartitionSpec as P

F32, BF16 = jnp.float32, jnp.bfloat16
BLK, HG, SLOTS, TQ = 512, 8, 5, 256
XR = 272
LOG2E = 1.4426950408889634
SC = LOG2E / math.sqrt(128.0)
BIG = 1e30
EPS = 1e-05
NT = (((1,), (1,)), ((), ()))
MESH = pl.DeviceIdType.MESH


def dot_nt(a, b):
    return lax.dot_general(a, b, NT, preferred_element_type=F32)


def dot(a, b):
    return jnp.dot(a, b, preferred_element_type=F32)


def fold_sum(x):
    return jnp.sum(x.reshape(x.shape[0] // 8, 8, x.shape[1]), axis=0)


def fold_max(x):
    return jnp.max(jnp.max(x.reshape(x.shape[0] // 8, 8, x.shape[1]), axis=0), axis=0, keepdims=True)


def prefix_sums(x):
    lane = lax.broadcasted_iota(jnp.int32, x.shape, 1)
    step = 1
    while step < x.shape[1]:
        x = x + jnp.where(lane >= step, pltpu.roll(x, step, 1), 0.0)
        step *= 2
    return x


def to_columns(rows):
    wide = jnp.concatenate([rows, jnp.zeros((128 - rows.shape[0], rows.shape[1]), F32)], axis=0)
    return jnp.transpose(wide)


def t16(x):
    return jnp.transpose(x.astype(F32)).astype(BF16)


class Refs:
    pass


class Place:
    def __init__(self):
        self.s, self.hd = lax.axis_index("seq"), lax.axis_index("head")
        self.z, self.col = self.s // 2, self.s % 2
        self.g, self.c = self.hd // 2, self.hd % 2
        self.sibling = (self.s, self.g * 2 + 1 - self.c)
        self.beside = (self.z * 2 + 1 - self.col, self.hd)
        self.above = (self.s + 2, self.hd)
        self.below = (self.s - 2, self.hd)


def remote(src, dst, send, recv, device):
    return pltpu.make_async_remote_copy(
        src_ref=src, dst_ref=dst, send_sem=send, recv_sem=recv, device_id=device, device_id_type=MESH)


def greet(w):
    barrier = pltpu.get_barrier_semaphore()

    def tell(device):
        pl.semaphore_signal(barrier, inc=1, device_id=device, device_id_type=MESH)

    def others(k, _):
        tell((w.s, (w.hd + k) % 16))
        return 0
    lax.fori_loop(1, 16, others, 0)
    tell(w.beside)

    @pl.when(w.z < 3)
    def _():
        tell(w.above)

    @pl.when(w.z > 0)
    def _():
        tell(w.below)
    pl.semaphore_wait(barrier, 16 + (w.z + 2) // 3 + (5 - w.z) // 3 - 0)


def swap_copies(r, w):
    return (remote(r.query.at[1 - w.c], r.qraw.at[1], r.swap_send.at[0], r.swap_recv.at[0], w.sibling),
            remote(r.decay.at[1 - w.c], r.decay_raw.at[1], r.swap_send.at[1], r.swap_recv.at[1], w.sibling))


def spread(p):
    return (p % 256) // 32 * 64 + p // 256 * 32 + p % 32


CHUNKS = [(spread(32 * i), 32 * i) for i in range(16)]


def part(r, slot, j):
    return r.aux.at[slot] if j == 3 else r.kvb.at[slot, j]


def up_copy(r, w, step, j):
    return remote(part(r, 2 * step, j), part(r, 2 * step + 2, j), r.up_send.at[step, j], r.up_recv.at[step, j], w.above)


def side_copy(r, w, step, j):
    return remote(part(r, 2 * step + 2 * w.col, j), part(r, 2 * step + 1, j), r.side_send.at[step, j], r.side_recv.at[step, j], w.beside)


def sends_up(w, step):
    return (w.z < 3) if step == 0 else ((w.z >= 1) & (w.z < 3))


def sends_side(w, step):
    return w.z >= step + w.col


def gets_up(w, step):
    return w.z >= step + 1


def gets_side(w, step):
    return w.z >= step + 1 - w.col


def load_own(r, w):
    loads = [pltpu.make_async_copy(ref.at[w.c], r.raw.at[i], r.load_sem.at[i])
             for i, ref in enumerate((r.key, r.value, r.inner, r.outer))]
    qload = pltpu.make_async_copy(r.query.at[w.c], r.qraw.at[0], r.load_sem.at[4])
    aload = pltpu.make_async_copy(r.decay.at[w.c], r.decay_raw.at[0], r.load_sem.at[5])
    aload.start()
    for x in loads:
        x.start()
    qload.start()
    greet(w)
    swaps = swap_copies(r, w)
    swaps[1].start()
    swaps[0].start()

    def send_part(j):
        @pl.when(sends_up(w, 0))
        def _():
            up_copy(r, w, 0, j).start()

        @pl.when((w.col == 0) & sends_side(w, 0))
        def _():
            side_copy(r, w, 0, j).start()

    for i in range(4):
        loads[i].wait()
        r.wide[...] = r.raw[i].astype(F32)
        if i < 3:
            r.kvb[0, i] = r.wide[pl.ds(w.g, BLK, stride=8), :].astype(BF16)
            send_part(i)
        else:
            for pos, to in CHUNKS:
                r.outer_own[to:to + 32, :] = r.wide[pl.ds(w.g + 8 * pos, 32, stride=8), :].astype(BF16)
    aload.wait()
    swaps[1].wait_recv()
    mine, theirs = r.decay_raw[0], r.decay_raw[1]
    first = jnp.where(w.c == 0, mine, theirs)
    second = jnp.where(w.c == 0, theirs, mine)
    r.aux[0, 0:8, :] = jnp.concatenate([first, second], axis=0)
    docs = jnp.where(w.c == 0, r.docs[0:1, :], r.docs[1:2, :]).astype(F32)
    r.aux[0, 8:16, :] = jnp.broadcast_to(docs, (8, BLK))
    send_part(3)
    qload.wait()
    swaps[0].wait_recv()
    for i in range(2):
        r.wide[0:2048, :] = r.qraw[i].astype(F32)
        base = 4 * w.c if i == 0 else 4 - 4 * w.c
        for j in range(4):
            for pos, to in CHUNKS:
                r.q[base + j, to:to + 32, :] = r.wide[pl.ds(j + 4 * pos, 32, stride=4), :].astype(BF16)
    for x in swaps:
        x.wait_send()


def take_up(r, w, step, parts):
    @pl.when(gets_up(w, step))
    def _():
        for j in parts:
            up_copy(r, w, step, j).wait_recv()
            if step == 0:
                @pl.when(sends_up(w, 1))
                def _():
                    up_copy(r, w, 1, j).start()

                side_copy(r, w, 1 - w.col, j).start()
            else:
                @pl.when(w.col == 1)
                def _():
                    side_copy(r, w, 1, j).start()


def take_side(r, w, step, parts):
    for j in parts:
        side_copy(r, w, step, j).wait_recv()


def end_sends(r, w):
    for step in range(2):
        @pl.when(sends_up(w, step))
        def _():
            for j in range(4):
                up_copy(r, w, step, j).wait_send()

        @pl.when(sends_side(w, step))
        def _():
            for j in range(4):
                side_copy(r, w, step, j).wait_send()


def own_prepare(r):
    own = prefix_sums(r.aux[0, 0:8, :]) * LOG2E
    cols = to_columns(jnp.concatenate([own, r.aux[0, 8:16, :]], axis=0))
    r.csum_col[...] = cols
    rows = jnp.transpose(jnp.concatenate([cols[pos:pos + 32] for pos, _ in CHUNKS], axis=0))
    r.csum[...] = rows[0:8]
    r.docq[...] = rows[8:16]
    doc_c = cols[:, 8:9]
    cb = dot_nt(r.kvb[0, 2], r.outer_own[...])
    kj = lax.broadcasted_iota(jnp.int32, (BLK, BLK), 0)
    qi = spread(lax.broadcasted_iota(jnp.int32, (BLK, BLK), 1))
    seen = (qi >= kj) & (doc_c == r.docq[0:1, :])
    r.cb[...] = jnp.where(seen, cb, 0.0)
    r.hide[...] = jnp.where(seen, 0.0, -BIG)
    for slot in range(SLOTS):
        r.vt[slot, 128:144, :] = jnp.ones((16, BLK), BF16)
    r.vt[0, 0:128, :] = t16(r.kvb[0, 1])


def late(x):
    return jnp.concatenate([jnp.zeros_like(x), x], axis=1)


def own_half(r, qt, polls=()):
    base = qt * TQ
    parts = ((slice(0, 256), slice(0, 256)), (slice(256, 512), slice(128, 256)))
    cols = slice(base, base + TQ)
    polls = dict(polls)
    for at in range(2):
        r.pbuf[at, 256:512, 0:128] = jnp.zeros((256, 128), BF16)
        r.mbuf[at, 256:512, 0:128] = jnp.zeros((256, 128), BF16)

    def score(h):
        tops = []
        for keys, part_cols in parts:
            here = slice(base + part_cols.start, base + part_cols.stop)
            s = dot_nt(r.kvb[0, 0, keys, :], r.q[h, here, :]) + r.hide[keys, here]
            r.sbuf[h % 2, keys, part_cols] = s
            tops.append(jnp.max(s.reshape(32, 8, s.shape[1]), axis=0))
        both = jnp.concatenate([tops[0][:, 0:128], jnp.maximum(tops[0][:, 128:256], tops[1])], axis=1)
        return jnp.max(both, axis=0, keepdims=True)

    def soft(h, m):
        r.m[h, :, cols] = jnp.broadcast_to(m, (8, TQ))
        sums = []
        for keys, part_cols in parts:
            here = slice(base + part_cols.start, base + part_cols.stop)
            p = jnp.exp2((r.sbuf[h % 2, keys, part_cols] - m[:, part_cols]) * SC)
            fall = jnp.minimum(r.csum[h:h + 1, here] - r.csum_col[keys, h:h + 1], 0.0)
            mix = jnp.exp2(fall) * r.cb[keys, here]
            sums.append((fold_sum(p * p), fold_sum(p * mix), fold_sum(mix * mix)))
            r.pbuf[h % 2, keys, part_cols] = p.astype(BF16)
            r.mbuf[h % 2, keys, part_cols] = mix.astype(BF16)
        r.sq[h, :, cols], r.cross[h, :, cols], r.mixsq[h, :, cols] = (x + late(y) for x, y in zip(*sums))

    def apply(h):
        r.acc[h, 0:144, cols] = dot(r.vt[0], r.pbuf[h % 2])
        r.acc[h, 144:XR, cols] = jnp.zeros((128, TQ), F32)
        r.stud[h, :, cols] = dot(r.vt[0, 0:128, :], r.mbuf[h % 2])
        if qt == 0:
            r.state[h] = jnp.zeros((256, 128), F32)

    top = score(0)
    for h in range(HG):
        now = top
        if h + 1 < HG:
            top = score(h + 1)
        soft(h, now)
        if h > 0:
            apply(h - 1)
        if h in polls:
            polls[h]()
    apply(HG - 1)


def prepare(r, slot):
    sums = prefix_sums(r.aux[slot, 0:8, :])
    whole = sums[:, BLK - 1:BLK]
    doc_last = r.aux[1, 8:9, BLK - 1:BLK]
    tail = jnp.zeros((8, 1), F32)
    for t in range(1, slot):
        tail = tail + jnp.sum(r.aux[t, 0:8, :], axis=1, keepdims=True)
    weight = jnp.exp(whole - sums + tail)
    r.bdec[...] = jnp.where(r.aux[slot, 8:9, :] == doc_last, weight, 0.0)
    doc_c = to_columns(r.aux[slot, 8:16, :])[:, 0:1]
    r.kmask[slot] = jnp.broadcast_to(jnp.where(doc_c == doc_last, 0.0, -BIG), (BLK, 128))
    r.qoff[...] = jnp.broadcast_to(jnp.where(r.docq[0:1, :] == doc_last, 0.0, -BIG), (8, BLK))
    r.vt[slot, 0:128, :] = t16(r.kvb[slot, 1])
    r.bt[...] = jnp.transpose(r.kvb[slot, 2].astype(F32))


def slot_half(r, slot, qt, first, polls=()):
    cols = slice(qt * TQ, (qt + 1) * TQ)

    def score(h):
        mx = None
        for c in range(2):
            keys = slice(c * 256, c * 256 + 256)
            km = r.kmask[slot, keys, :]
            s = dot_nt(r.kvb[slot, 0, keys, :], r.q[h, cols, :]) + jnp.concatenate([km] * (TQ // 128), axis=1)
            r.sbuf[h % 2, keys, :] = s
            top = jnp.max(s.reshape(32, 8, TQ), axis=0)
            mx = top if mx is None else jnp.maximum(mx, top)
        return jnp.max(mx, axis=0, keepdims=True)

    def soft(h, top):
        qoff = r.qoff[0:1, cols]
        m_old = r.m[h, 0:1, cols]
        m = jnp.maximum(m_old, top + qoff)
        f = jnp.exp2((m_old - m) * SC)
        low = m - qoff
        r.m[h, :, cols] = jnp.broadcast_to(m, (8, TQ))
        r.cross[h, :, cols] = r.cross[h, :, cols] * f
        sq = r.sq[h, :, cols] * (f * f)
        for c in range(2):
            keys = slice(c * 256, c * 256 + 256)
            p = jnp.exp2((r.sbuf[h % 2, keys, :] - low) * SC)
            sq = sq + fold_sum(p * p)
            r.pbuf[h % 2, keys, :] = p.astype(BF16)
        r.sq[h, :, cols] = sq
        return f

    def extend(h):
        xb = (r.bt[...] * r.bdec[h:h + 1, :]).astype(BF16)
        r.xb[slot, h] = xb
        r.state[h] = r.state[h] + dot_nt(jnp.concatenate([r.vt[slot, 0:128, :], xb], axis=0), xb)

    def apply(h, f):
        both = jnp.concatenate([r.vt[slot], r.xb[slot, h]], axis=0)
        r.acc[h, :, cols] = r.acc[h, :, cols] * f + dot(both, r.pbuf[h % 2])

    polls = dict(polls)
    top = score(0)
    kept = None
    for h in range(HG):
        now = top
        if h + 1 < HG:
            top = score(h + 1)
        f = soft(h, now)
        if first:
            extend(h)
        if h > 0:
            apply(h - 1, kept)
        kept = f
        if h in polls:
            polls[h]()
    apply(HG - 1, kept)


def finish_rows(r, w, qt):
    cols = slice(qt * TQ, (qt + 1) * TQ)
    doc_last = r.aux[1, 8:9, BLK - 1:BLK]
    r.from_prev[...] = jnp.where((r.docq[0:1, cols] == doc_last) & (w.s > 0), jnp.ones((8, TQ), F32), 0.0)
    r.ct[...] = jnp.transpose(r.outer_own[cols, :].astype(F32))
    r.ssq[qt] = jnp.zeros((8, TQ), F32)

    def head(i, _):
        for u in range(2):
            h = i * 2 + u
            a = jnp.exp2(r.csum[pl.ds(h, 1), cols]) * r.from_prev[0:1, :]
            y = dot_nt(r.state[h].astype(BF16), r.outer_own[cols, :])
            inv = 1.0 / r.acc[h, 128:129, cols]
            tf = r.acc[h, 0:128, cols] * inv
            sf = r.stud[h, :, cols] + a * y[0:128, :]
            r.acc[h, 0:128, cols] = tf
            r.stud[h, :, cols] = sf
            r.mixsq[h, :, cols] = (r.mixsq[h, :, cols] + (a * a) * fold_sum(y[128:256, :] * r.ct[...])
                                   - (2.0 * inv) * (r.cross[h, :, cols] + a * fold_sum(r.ct[...] * r.acc[h, 144:XR, cols]))
                                   + (inv * inv) * r.sq[h, :, cols])
            r.ssq[qt, 0:1, :] = r.ssq[qt, 0:1, :] + jnp.sum(fold_sum(tf * tf), axis=0, keepdims=True)
            r.ssq[qt, 1:2, :] = r.ssq[qt, 1:2, :] + jnp.sum(fold_sum(sf * sf), axis=0, keepdims=True)
        return 0
    lax.fori_loop(0, HG // 2, head, 0)


def finish_layout(r, qt):
    cols = slice(qt * TQ, (qt + 1) * TQ)

    def head(h, _):
        r.teach[h, cols, :] = jnp.transpose(r.acc[h, 0:128, cols]).astype(BF16)
        r.student[h, cols, :] = jnp.transpose(r.stud[h, :, cols]).astype(BF16)
        r.err[pl.ds(h, 1), cols] = jnp.sum(r.mixsq[h, :, cols], axis=0, keepdims=True)
        return 0
    lax.fori_loop(0, HG, head, 0)


def ssq_copy(r, w, qt, k):
    return remote(r.ssq.at[qt], r.ssq_all.at[qt, w.g], r.ssq_send.at[qt, k], r.ssq_recv.at[qt, w.g],
                  (w.s, ((w.g + k) % 8) * 2 + w.c))


def ssq_from(r, w, qt, k):
    g = (w.g + 8 - k) % 8
    return remote(r.ssq.at[qt], r.ssq_all.at[qt, g], r.ssq_send.at[qt, k], r.ssq_recv.at[qt, g], (w.s, g * 2 + w.c))


def send_ssq(r, w, qt):
    for k in range(1, 8):
        ssq_copy(r, w, qt, k).start()
    r.ssq_all[qt, pl.ds(w.g, 1)] = r.ssq[qt].reshape(1, 8, TQ)


def gap_rows(qt, chip):
    return pl.ds(pl.multiple_of(qt * TQ + chip * 32, 32), 32)


def gap_lanes(g):
    return pl.ds(pl.multiple_of(g * 1024, 1024), 1024)


def gap_copy(r, w, qt, chip):
    to = chip * 2 + qt
    return remote(r.gap.at[gap_rows(qt, chip)], r.out.at[w.c, :, gap_lanes(w.g)],
                  r.out_send.at[to], r.out_recv.at[w.hd], (w.s, to))


def gap_stay(r, w):
    return pltpu.make_async_copy(r.gap.at[gap_rows(w.c, w.g)], r.out.at[w.c, :, gap_lanes(w.g)], r.out_send.at[w.hd])


def send_gap(r, w, qt):
    for k in range(1, 8):
        ssq_from(r, w, qt, k).wait_recv()
    sums = jnp.sum(r.ssq_all[qt], axis=0)
    r.scale[...] = to_columns(lax.rsqrt(sums / (8.0 * HG * 128) + EPS))
    gain = r.gain[pl.ds(pl.multiple_of(w.g * 1024, 1024), 1024)].reshape(1, 1024)

    def one(k, _):
        chip = (w.g + k) % 8
        rows = gap_rows(qt, chip)
        scale = r.scale[pl.ds(pl.multiple_of(chip * 32, 32), 32), :]
        t_scale, s_scale = scale[:, 0:1], scale[:, 1:2]
        for h in range(HG):
            lanes = slice(h * 128, (h + 1) * 128)
            gap = gain[:, lanes] * r.student[h, rows, :].astype(F32) * s_scale - r.teach[h, rows, :].astype(F32) * t_scale
            r.gap[rows, lanes] = gap.astype(BF16)
        stays = (k == 8) & (w.c == qt)

        @pl.when(stays)
        def _():
            gap_stay(r, w).start()

        @pl.when(jnp.logical_not(stays))
        def _():
            gap_copy(r, w, qt, chip).start()
        return 0
    lax.fori_loop(1, 9, one, 0)


def err_copy(r, w, seq):
    return remote(r.err_pair.at[1], r.err_out.at[seq], r.swap_send.at[2], r.swap_recv.at[2], w.sibling)


def send_err(r, w):
    cols = to_columns(r.err[...])
    back = sorted((pos, at) for pos, at in CHUNKS)
    err = jnp.transpose(jnp.concatenate([cols[at:at + 32] for _, at in back], axis=0))
    top, bottom = err[0:4, :], err[4:8, :]
    r.err_pair[0] = jnp.where(w.c == 0, top, bottom)
    r.err_pair[1] = jnp.where(w.c == 0, bottom, top)
    err_copy(r, w, w.c).start()
    near = pltpu.make_async_copy(r.err_pair.at[0], r.err_out.at[w.c], r.load_sem.at[0])
    near.start()
    near.wait()


def end_share(r, w):
    gap_stay(r, w).wait()
    err_copy(r, w, w.c).wait_send()
    err_copy(r, w, 1 - w.c).wait_recv()
    for k in range(1, 8):
        for qt in range(2):
            ssq_copy(r, w, qt, k).wait_send()

    def arrived(k, _):
        sender = (w.hd + k) % 16
        remote(r.gap.at[0:32], r.out.at[sender % 2, :, gap_lanes(sender // 2)],
               r.out_send.at[sender], r.out_recv.at[sender], (w.s, sender)).wait_recv()
        gap_copy(r, w, sender % 2, sender // 2).wait_send()
        return 0
    lax.fori_loop(1, 16, arrived, 0)


ARGS = ("query", "key", "value", "inner", "outer", "decay", "docs", "gain")
OUTS = ("out", "err_out")
DMA = pltpu.SemaphoreType.DMA
SCRATCH = dict(
    qraw=pltpu.VMEM((2, 2048, 128), BF16), decay_raw=pltpu.VMEM((2, 4, BLK), F32),
    raw=pltpu.VMEM((4, 4096, 128), BF16), wide=pltpu.VMEM((4096, 128), F32),
    q=pltpu.VMEM((HG, BLK, 128), BF16), kvb=pltpu.VMEM((SLOTS, 3, BLK, 128), BF16),
    aux=pltpu.VMEM((SLOTS, 16, BLK), F32), outer_own=pltpu.VMEM((BLK, 128), BF16),
    csum=pltpu.VMEM((8, BLK), F32), csum_col=pltpu.VMEM((BLK, 128), F32), docq=pltpu.VMEM((8, BLK), F32),
    cb=pltpu.VMEM((BLK, BLK), F32), hide=pltpu.VMEM((BLK, BLK), F32),
    m=pltpu.VMEM((HG, 8, BLK), F32), sq=pltpu.VMEM((HG, 8, BLK), F32),
    cross=pltpu.VMEM((HG, 8, BLK), F32), mixsq=pltpu.VMEM((HG, 8, BLK), F32),
    acc=pltpu.VMEM((HG, XR, BLK), F32), stud=pltpu.VMEM((HG, 128, BLK), F32),
    state=pltpu.VMEM((HG, 256, 128), F32), bdec=pltpu.VMEM((8, BLK), F32),
    kmask=pltpu.VMEM((SLOTS, BLK, 128), F32), qoff=pltpu.VMEM((8, BLK), F32),
    vt=pltpu.VMEM((SLOTS, 144, BLK), BF16), xb=pltpu.VMEM((SLOTS, HG, 128, BLK), BF16), bt=pltpu.VMEM((128, BLK), F32),
    sbuf=pltpu.VMEM((2, BLK, TQ), F32), pbuf=pltpu.VMEM((2, BLK, TQ), BF16), mbuf=pltpu.VMEM((2, BLK, TQ), BF16),
    ct=pltpu.VMEM((128, TQ), F32), from_prev=pltpu.VMEM((8, TQ), F32), scale=pltpu.VMEM((TQ, 128), F32),
    teach=pltpu.VMEM((HG, BLK, 128), BF16), student=pltpu.VMEM((HG, BLK, 128), BF16),
    err=pltpu.VMEM((8, BLK), F32), err_pair=pltpu.VMEM((2, 4, BLK), F32),
    ssq=pltpu.VMEM((2, 8, TQ), F32), ssq_all=pltpu.VMEM((2, 8, 8, TQ), F32), gap=pltpu.VMEM((BLK, HG * 128), BF16),
    load_sem=DMA((6,)), swap_send=DMA((3,)), swap_recv=DMA((3,)),
    up_send=DMA((2, 4)), up_recv=DMA((2, 4)), side_send=DMA((2, 4)), side_recv=DMA((2, 4)),
    ssq_send=DMA((2, 8)), ssq_recv=DMA((2, 8)), out_send=DMA((16,)), out_recv=DMA((16,)),
)


def kernel(*refs):
    r = Refs()
    for name, ref in zip(ARGS + OUTS + tuple(SCRATCH), refs):
        setattr(r, name, ref)
    w = Place()
    load_own(r, w)
    own_prepare(r)
    own_half(r, 0, {2: lambda: take_up(r, w, 0, (0,)), 7: lambda: take_up(r, w, 0, (1,))})
    own_half(r, 1, {5: lambda: take_up(r, w, 0, (2, 3))})

    @pl.when(w.s == 0)
    def _():
        r.aux[1] = jnp.zeros((16, BLK), F32)

    @pl.when(gets_side(w, 0))
    def _():
        side_copy(r, w, 0, 3).wait_recv()

    @pl.when(w.s >= 2)
    def _():
        prepare(r, 2)
        slot_half(r, 2, 0, True, {3: lambda: take_up(r, w, 1, (0,))})
        slot_half(r, 2, 1, False, {5: lambda: take_up(r, w, 1, (1,))})

    @pl.when(w.s >= 1)
    def _():
        take_side(r, w, 0, (0, 1, 2))
        prepare(r, 1)
        slot_half(r, 1, 0, True, {2: lambda: take_up(r, w, 1, (2, 3))})

    @pl.when(w.s >= 3)
    def _():
        take_side(r, w, 1, (3,))

    @pl.when(w.s >= 4)
    def _():
        prepare(r, 4)
        slot_half(r, 4, 0, True)

    @pl.when(w.s >= 3)
    def _():
        take_side(r, w, 1, (0, 1, 2))
        prepare(r, 3)
        slot_half(r, 3, 0, True)
    finish_rows(r, w, 0)
    send_ssq(r, w, 0)
    finish_layout(r, 0)

    @pl.when(w.s >= 1)
    def _():
        slot_half(r, 1, 1, False)
    send_gap(r, w, 0)

    @pl.when(w.s >= 4)
    def _():
        slot_half(r, 4, 1, False)

    @pl.when(w.s >= 3)
    def _():
        slot_half(r, 3, 1, False)
    finish_rows(r, w, 1)
    send_ssq(r, w, 1)
    finish_layout(r, 1)
    send_err(r, w)
    send_gap(r, w, 1)
    end_share(r, w)
    end_sends(r, w)


def settle(out, err, out_to, err_to):
    out_to[...] = out[...]
    err_to[...] = err[...]


def on_device(query_rows, key_rows, value_rows, state_in, state_out, log_decay, doc_ids, norm_gain):
    flat = [x.reshape(2, -1, 128) for x in (query_rows, key_rows, value_rows, state_in, state_out)]
    shapes = (jax.ShapeDtypeStruct((2, 32, 8192), BF16), jax.ShapeDtypeStruct((2, 4, BLK), F32))
    anywhere = pl.BlockSpec(memory_space=pl.ANY)
    landed = pl.pallas_call(
        kernel,
        out_shape=shapes,
        in_specs=[pl.BlockSpec(memory_space=pl.ANY)] * 6 + [pl.BlockSpec(memory_space=pltpu.VMEM)] * 2,
        out_specs=(pl.BlockSpec(memory_space=pl.ANY), pl.BlockSpec(memory_space=pl.ANY)),
        scratch_shapes=list(SCRATCH.values()),
        compiler_params=pltpu.CompilerParams(collective_id=0, has_side_effects=True, vmem_limit_bytes=56 * 2**20),
        cost_estimate=pl.CostEstimate(flops=10**10, bytes_accessed=10**7, transcendentals=0),
    )(*flat, log_decay, doc_ids, norm_gain)
    half = pl.BlockSpec((1, 32, 8192), lambda i: (i, 0, 0))
    quarter = pl.BlockSpec((1, 4, BLK), lambda i: (i, 0, 0))
    return pl.pallas_call(
        settle,
        out_shape=shapes,
        grid=(2,),
        in_specs=[half, quarter],
        out_specs=(half, quarter),
    )(*landed)


def solution(mesh):
    placed = (
        P(None, "seq", "head", None),
        P(None, "seq", None, None),
        P(None, "seq", None, None),
        P(None, "seq", None, None),
        P(None, "seq", None, None),
        P(None, "head", "seq"),
        P(None, "seq"),
        P(),
    )
    return jax.shard_map(
        on_device,
        mesh=mesh,
        in_specs=placed,
        out_specs=(P(None, ("seq", "head"), None), P(None, "head", "seq")),
        check_vma=False,
    )
```

time: 74.2 us -> 67 us (0.903)
  Pallas kernels: 70 us -> 66.1 us
  local copies, waits for them, and re-layouts: 2.88 us -> 0 us
    pallas_call x1 -> x2, Pallas kernels: 70 us -> 66.1 us  [the longest x1 64 us: on_device(): pl.pallas_call(kernel, out_shape=shapes, in_specs=[pl.BlockSpec(memory_sp...]
    unnamed x4 -> x0, local copies, waits for them, and re-layouts: 2.88 us -> none
where the time goes in v3:
time: 67 us; the launch traced here: 66.7 us
  Pallas kernels  66.1 us (99%)
    pallas_call x1, Pallas kernels, on_device(): pl.pallas_call(kernel, out_shape=shapes, in_specs=[pl.BlockSpec(memory_sp...  64 us
    pallas_call x1, Pallas kernels, on_device(): pl.pallas_call(settle, out_shape=shapes, grid=(2,), in_specs=[half, quart...  2.07 us

profile of v3, /device:TPU:89, one launch (start us, length us, event | category | flops | bytes accessed | tf_op | source)
XLA Modules:
  0.0 66.7 jit_solution(10539373092483613820)
XLA Ops:
  0.6 64.0 %shard_map.95 = (bf16[2,32,8192]{2,1,0:T(8,128)(2,1)}, f32[2,4,512]{2,1,0:T(4,128)}) custom-call(bf16[2,2048,128]{2,1,0:T(8,128)(2,1)} %bitcast.9, bf16[2,4096,128]{2,1,0:T(8,128)(2,1)} %bitcast.5, bf16[2,4096,128]{2,1,0:T(8,128)(2,1)} %bitcast.6, bf16[2,4096,128]{2,1,0:T(8,128)(2,1)} %bitcast.7, bf16[2,4096,128]{2,1,0:T(8,128)(2,1)} %bitcast.8, ...), custom_call_target="tpu_custom_call" | custom-call | flops 10000000000 | bytes 10000000 | tf_op jit(solution)/shard_map/pallas_call | solution.py:613
  64.7 2.1 %shard_map.96 = (bf16[2,32,8192]{2,1,0:T(8,128)(2,1)}, f32[2,4,512]{2,1,0:T(4,128)}) custom-call(bf16[2,32,8192]{2,1,0:T(8,128)(2,1)} %get-tuple-element.4.out, f32[2,4,512]{2,1,0:T(4,128)} %get-tuple-element.5.err), custom_call_target="tpu_custom_call" | custom-call | tf_op jit(solution)/shard_map/pallas_call | solution.py:624

commit v4 on v3

--- a/solution.py
+++ b/solution.py
@@ -157,24 +157,28 @@
         def _():
             side_copy(r, w, 0, j).start()
 
+    def send_small():
+        aload.wait()
+        swaps[1].wait_recv()
+        mine, theirs = r.decay_raw[0], r.decay_raw[1]
+        first = jnp.where(w.c == 0, mine, theirs)
+        second = jnp.where(w.c == 0, theirs, mine)
+        r.aux[0, 0:8, :] = jnp.concatenate([first, second], axis=0)
+        docs = jnp.where(w.c == 0, r.docs[0:1, :], r.docs[1:2, :]).astype(F32)
+        r.aux[0, 8:16, :] = jnp.broadcast_to(docs, (8, BLK))
+        send_part(3)
+
     for i in range(4):
         loads[i].wait()
         r.wide[...] = r.raw[i].astype(F32)
         if i < 3:
             r.kvb[0, i] = r.wide[pl.ds(w.g, BLK, stride=8), :].astype(BF16)
             send_part(i)
+            if i == 0:
+                send_small()
         else:
             for pos, to in CHUNKS:
                 r.outer_own[to:to + 32, :] = r.wide[pl.ds(w.g + 8 * pos, 32, stride=8), :].astype(BF16)
-    aload.wait()
-    swaps[1].wait_recv()
-    mine, theirs = r.decay_raw[0], r.decay_raw[1]
-    first = jnp.where(w.c == 0, mine, theirs)
-    second = jnp.where(w.c == 0, theirs, mine)
-    r.aux[0, 0:8, :] = jnp.concatenate([first, second], axis=0)
-    docs = jnp.where(w.c == 0, r.docs[0:1, :], r.docs[1:2, :]).astype(F32)
-    r.aux[0, 8:16, :] = jnp.broadcast_to(docs, (8, BLK))
-    send_part(3)
     qload.wait()
     swaps[0].wait_recv()
     for i in range(2):
@@ -193,11 +197,17 @@
         for j in parts:
             up_copy(r, w, step, j).wait_recv()
             if step == 0:
+                @pl.when(w.col == 1)
+                def _():
+                    side_copy(r, w, 0, j).start()
+
                 @pl.when(sends_up(w, 1))
                 def _():
                     up_copy(r, w, 1, j).start()
 
-                side_copy(r, w, 1 - w.col, j).start()
+                @pl.when(w.col == 0)
+                def _():
+                    side_copy(r, w, 1, j).start()
             else:
                 @pl.when(w.col == 1)
                 def _():
@@ -314,17 +324,26 @@
 
 
 def slot_half(r, slot, qt, first, polls=()):
-    cols = slice(qt * TQ, (qt + 1) * TQ)
+    base = qt * TQ
+    cols = slice(base, base + TQ)
+    far = slot == SLOTS - 1
+    parts = ((slice(0, 256), slice(0, 128 if far else 256)), (slice(256, 512), slice(0, 256)))
+    if far:
+        for at in range(2):
+            r.pbuf[at, 0:256, 128:256] = jnp.zeros((256, 128), BF16)
 
     def score(h):
-        mx = None
-        for c in range(2):
-            keys = slice(c * 256, c * 256 + 256)
+        tops = []
+        for keys, part_cols in parts:
             km = r.kmask[slot, keys, :]
-            s = dot_nt(r.kvb[slot, 0, keys, :], r.q[h, cols, :]) + jnp.concatenate([km] * (TQ // 128), axis=1)
-            r.sbuf[h % 2, keys, :] = s
-            top = jnp.max(s.reshape(32, 8, TQ), axis=0)
-            mx = top if mx is None else jnp.maximum(mx, top)
+            s = dot_nt(r.kvb[slot, 0, keys, :], r.q[h, base:base + part_cols.stop, :])
+            s = s + jnp.concatenate([km] * (part_cols.stop // 128), axis=1)
+            r.sbuf[h % 2, keys, part_cols] = s
+            tops.append(jnp.max(s.reshape(32, 8, part_cols.stop), axis=0))
+        if far:
+            mx = jnp.concatenate([jnp.maximum(tops[0], tops[1][:, 0:128]), tops[1][:, 128:256]], axis=1)
+        else:
+            mx = jnp.maximum(*tops)
         return jnp.max(mx, axis=0, keepdims=True)
 
     def soft(h, top):
@@ -336,11 +355,13 @@
         r.m[h, :, cols] = jnp.broadcast_to(m, (8, TQ))
         r.cross[h, :, cols] = r.cross[h, :, cols] * f
         sq = r.sq[h, :, cols] * (f * f)
-        for c in range(2):
-            keys = slice(c * 256, c * 256 + 256)
-            p = jnp.exp2((r.sbuf[h % 2, keys, :] - low) * SC)
-            sq = sq + fold_sum(p * p)
-            r.pbuf[h % 2, keys, :] = p.astype(BF16)
+        for keys, part_cols in parts:
+            p = jnp.exp2((r.sbuf[h % 2, keys, part_cols] - low[:, part_cols]) * SC)
+            more = fold_sum(p * p)
+            if part_cols.stop < TQ:
+                more = jnp.concatenate([more, jnp.zeros_like(more)], axis=1)
+            sq = sq + more
+            r.pbuf[h % 2, keys, part_cols] = p.astype(BF16)
         r.sq[h, :, cols] = sq
         return f
 
@@ -539,8 +560,8 @@
     w = Place()
     load_own(r, w)
     own_prepare(r)
-    own_half(r, 0, {2: lambda: take_up(r, w, 0, (0,)), 7: lambda: take_up(r, w, 0, (1,))})
-    own_half(r, 1, {5: lambda: take_up(r, w, 0, (2, 3))})
+    own_half(r, 0, {4: lambda: take_up(r, w, 0, (0, 3))})
+    own_half(r, 1, {0: lambda: take_up(r, w, 0, (1,)), 7: lambda: take_up(r, w, 0, (2,))})
 
     @pl.when(w.s == 0)
     def _():
@@ -553,14 +574,15 @@
     @pl.when(w.s >= 2)
     def _():
         prepare(r, 2)
-        slot_half(r, 2, 0, True, {3: lambda: take_up(r, w, 1, (0,))})
-        slot_half(r, 2, 1, False, {5: lambda: take_up(r, w, 1, (1,))})
+        slot_half(r, 2, 0, True, {7: lambda: take_up(r, w, 1, (0, 3))})
+        slot_half(r, 2, 1, False, {7: lambda: take_up(r, w, 1, (1,))})
 
     @pl.when(w.s >= 1)
     def _():
         take_side(r, w, 0, (0, 1, 2))
         prepare(r, 1)
-        slot_half(r, 1, 0, True, {2: lambda: take_up(r, w, 1, (2, 3))})
+        slot_half(r, 1, 0, True)
+        slot_half(r, 1, 1, False, {0: lambda: take_up(r, w, 1, (2,))})
 
     @pl.when(w.s >= 3)
     def _():
@@ -580,14 +602,13 @@
     send_ssq(r, w, 0)
     finish_layout(r, 0)
 
-    @pl.when(w.s >= 1)
-    def _():
-        slot_half(r, 1, 1, False)
-    send_gap(r, w, 0)
-
     @pl.when(w.s >= 4)
     def _():
-        slot_half(r, 4, 1, False)
+        slot_half(r, 4, 1, False, {4: lambda: send_gap(r, w, 0)})
+
+    @pl.when(w.s < 4)
+    def _():
+        send_gap(r, w, 0)
 
     @pl.when(w.s >= 3)
     def _():
@@ -601,33 +622,19 @@
     end_sends(r, w)
 
 
-def settle(out, err, out_to, err_to):
-    out_to[...] = out[...]
-    err_to[...] = err[...]
-
-
 def on_device(query_rows, key_rows, value_rows, state_in, state_out, log_decay, doc_ids, norm_gain):
     flat = [x.reshape(2, -1, 128) for x in (query_rows, key_rows, value_rows, state_in, state_out)]
     shapes = (jax.ShapeDtypeStruct((2, 32, 8192), BF16), jax.ShapeDtypeStruct((2, 4, BLK), F32))
-    anywhere = pl.BlockSpec(memory_space=pl.ANY)
     landed = pl.pallas_call(
         kernel,
-        out_shape=shapes,
+        out_shape=(pltpu.VMEM(shapes[0].shape, BF16), shapes[1]),
         in_specs=[pl.BlockSpec(memory_space=pl.ANY)] * 6 + [pl.BlockSpec(memory_space=pltpu.VMEM)] * 2,
-        out_specs=(pl.BlockSpec(memory_space=pl.ANY), pl.BlockSpec(memory_space=pl.ANY)),
+        out_specs=(pl.BlockSpec(memory_space=pltpu.VMEM), pl.BlockSpec(memory_space=pl.ANY)),
         scratch_shapes=list(SCRATCH.values()),
         compiler_params=pltpu.CompilerParams(collective_id=0, has_side_effects=True, vmem_limit_bytes=56 * 2**20),
         cost_estimate=pl.CostEstimate(flops=10**10, bytes_accessed=10**7, transcendentals=0),
     )(*flat, log_decay, doc_ids, norm_gain)
-    half = pl.BlockSpec((1, 32, 8192), lambda i: (i, 0, 0))
-    quarter = pl.BlockSpec((1, 4, BLK), lambda i: (i, 0, 0))
-    return pl.pallas_call(
-        settle,
-        out_shape=shapes,
-        grid=(2,),
-        in_specs=[half, quarter],
-        out_specs=(half, quarter),
-    )(*landed)
+    return landed
 
 
 def solution(mesh):

time: 67 us -> 61.4 us (0.916)
  Pallas kernels: 66.1 us -> 58.9 us
  local copies, waits for them, and re-layouts: 0 us -> 1.58 us
    pallas_call x2 -> x1, Pallas kernels: 66.1 us -> 58.9 us  [on_device(): pl.pallas_call(kernel, out_shape=(pltpu.VMEM(shapes[0].shape, BF16), shap...]
    unnamed x0 -> x4, local copies, waits for them, and re-layouts: none -> 1.58 us
where the time goes in v4:
time: 61.4 us; the launch traced here: 61.1 us
  Pallas kernels  58.9 us (96%)
  local copies, waits for them, and re-layouts  1.58 us (3%)
  between operations  0.65 us (1%)
    pallas_call x1, Pallas kernels, on_device(): pl.pallas_call(kernel, out_shape=(pltpu.VMEM(shapes[0].shape, BF16), shap...  58.9 us
    unnamed x4, local copies, waits for them, and re-layouts  1.58 us

profile of v4, /device:TPU:89, one launch (start us, length us, event | category | flops | bytes accessed | tf_op | source)
XLA Modules:
  0.0 61.1 jit_solution(6985838606644582412)
XLA Ops:
  0.6 58.9 %shard_map.95 = (bf16[2,32,8192]{2,1,0:T(8,128)(2,1)S(1)}, f32[2,4,512]{2,1,0:T(4,128)}) custom-call(bf16[2,2048,128]{2,1,0:T(8,128)(2,1)} %bitcast.9, bf16[2,4096,128]{2,1,0:T(8,128)(2,1)} %bitcast.5, bf16[2,4096,128]{2,1,0:T(8,128)(2,1)} %bitcast.6, bf16[2,4096,128]{2,1,0:T(8,128)(2,1)} %bitcast.7, bf16[2,4096,128]{2,1,0:T(8,128)(2,1)} %bitcast.8, ...), custom_call_target="tpu_custom_call" | custom-call | flops 10000000000 | bytes 10000000 | tf_op jit(solution)/shard_map/pallas_call | solution.py:628
  59.5 0.0 copy-start
  59.6 1.0 %copy.12 = bf16[2,32,8192]{2,1,0:T(8,128)(2,1)} copy(bf16[2,32,8192]{2,1,0:T(8,128)(2,1)S(1)} %get-tuple-element.2) | data formatting | bytes 2097152
  60.5 0.0 copy-done
  60.5 0.6 copy.13
Async XLA Ops:
  59.5 1.0 %copy-start = (f32[2,4,512]{2,1,0:T(4,128)S(1)}, f32[2,4,512]{2,1,0:T(4,128)}, u32[]{:S(2)}) copy-start(f32[2,4,512]{2,1,0:T(4,128)} %get-tuple-element.7) | copy-start | bytes 49156

commit v5 on v4

--- a/solution.py
+++ b/solution.py
@@ -49,7 +49,7 @@
 
 
 def t16(x):
-    return jnp.transpose(x.astype(F32)).astype(BF16)
+    return jnp.transpose(x)
 
 
 class Refs:
@@ -91,7 +91,10 @@
     @pl.when(w.z > 0)
     def _():
         tell(w.below)
-    pl.semaphore_wait(barrier, 16 + (w.z + 2) // 3 + (5 - w.z) // 3 - 0)
+
+
+def await_greetings(w):
+    pl.semaphore_wait(pltpu.get_barrier_semaphore(), 16 + (w.z + 2) // 3 + (5 - w.z) // 3)
 
 
 def swap_copies(r, w):
@@ -145,8 +148,6 @@
     qload.start()
     greet(w)
     swaps = swap_copies(r, w)
-    swaps[1].start()
-    swaps[0].start()
 
     def send_part(j):
         @pl.when(sends_up(w, 0))
@@ -173,7 +174,12 @@
         r.wide[...] = r.raw[i].astype(F32)
         if i < 3:
             r.kvb[0, i] = r.wide[pl.ds(w.g, BLK, stride=8), :].astype(BF16)
+            if i == 0:
+                await_greetings(w)
+                swaps[1].start()
             send_part(i)
+            if i == 0:
+                swaps[0].start()
             if i == 0:
                 send_small()
         else:
@@ -320,7 +326,7 @@
     r.kmask[slot] = jnp.broadcast_to(jnp.where(doc_c == doc_last, 0.0, -BIG), (BLK, 128))
     r.qoff[...] = jnp.broadcast_to(jnp.where(r.docq[0:1, :] == doc_last, 0.0, -BIG), (8, BLK))
     r.vt[slot, 0:128, :] = t16(r.kvb[slot, 1])
-    r.bt[...] = jnp.transpose(r.kvb[slot, 2].astype(F32))
+    r.bt[...] = t16(r.kvb[slot, 2]).astype(F32)
 
 
 def slot_half(r, slot, qt, first, polls=()):
@@ -338,7 +344,7 @@
             km = r.kmask[slot, keys, :]
             s = dot_nt(r.kvb[slot, 0, keys, :], r.q[h, base:base + part_cols.stop, :])
             s = s + jnp.concatenate([km] * (part_cols.stop // 128), axis=1)
-            r.sbuf[h % 2, keys, part_cols] = s
+            r.sbuf[h % 3, keys, part_cols] = s
             tops.append(jnp.max(s.reshape(32, 8, part_cols.stop), axis=0))
         if far:
             mx = jnp.concatenate([jnp.maximum(tops[0], tops[1][:, 0:128]), tops[1][:, 128:256]], axis=1)
@@ -356,7 +362,7 @@
         r.cross[h, :, cols] = r.cross[h, :, cols] * f
         sq = r.sq[h, :, cols] * (f * f)
         for keys, part_cols in parts:
-            p = jnp.exp2((r.sbuf[h % 2, keys, part_cols] - low[:, part_cols]) * SC)
+            p = jnp.exp2((r.sbuf[h % 3, keys, part_cols] - low[:, part_cols]) * SC)
             more = fold_sum(p * p)
             if part_cols.stop < TQ:
                 more = jnp.concatenate([more, jnp.zeros_like(more)], axis=1)
@@ -375,13 +381,12 @@
         r.acc[h, :, cols] = r.acc[h, :, cols] * f + dot(both, r.pbuf[h % 2])
 
     polls = dict(polls)
-    top = score(0)
+    ahead = [score(h) for h in range(1 if first else 2)]
     kept = None
     for h in range(HG):
-        now = top
-        if h + 1 < HG:
-            top = score(h + 1)
-        f = soft(h, now)
+        if h + len(ahead) < HG:
+            ahead.append(score(h + len(ahead)))
+        f = soft(h, ahead.pop(0))
         if first:
             extend(h)
         if h > 0:
@@ -396,7 +401,7 @@
     cols = slice(qt * TQ, (qt + 1) * TQ)
     doc_last = r.aux[1, 8:9, BLK - 1:BLK]
     r.from_prev[...] = jnp.where((r.docq[0:1, cols] == doc_last) & (w.s > 0), jnp.ones((8, TQ), F32), 0.0)
-    r.ct[...] = jnp.transpose(r.outer_own[cols, :].astype(F32))
+    r.ct[...] = t16(r.outer_own[cols, :]).astype(F32)
     r.ssq[qt] = jnp.zeros((8, TQ), F32)
 
     def head(i, _):
@@ -422,8 +427,8 @@
     cols = slice(qt * TQ, (qt + 1) * TQ)
 
     def head(h, _):
-        r.teach[h, cols, :] = jnp.transpose(r.acc[h, 0:128, cols]).astype(BF16)
-        r.student[h, cols, :] = jnp.transpose(r.stud[h, :, cols]).astype(BF16)
+        r.teach[h, cols, :] = t16(r.acc[h, 0:128, cols].astype(BF16))
+        r.student[h, cols, :] = t16(r.stud[h, :, cols].astype(BF16))
         r.err[pl.ds(h, 1), cols] = jnp.sum(r.mixsq[h, :, cols], axis=0, keepdims=True)
         return 0
     lax.fori_loop(0, HG, head, 0)
@@ -542,7 +547,7 @@
     state=pltpu.VMEM((HG, 256, 128), F32), bdec=pltpu.VMEM((8, BLK), F32),
     kmask=pltpu.VMEM((SLOTS, BLK, 128), F32), qoff=pltpu.VMEM((8, BLK), F32),
     vt=pltpu.VMEM((SLOTS, 144, BLK), BF16), xb=pltpu.VMEM((SLOTS, HG, 128, BLK), BF16), bt=pltpu.VMEM((128, BLK), F32),
-    sbuf=pltpu.VMEM((2, BLK, TQ), F32), pbuf=pltpu.VMEM((2, BLK, TQ), BF16), mbuf=pltpu.VMEM((2, BLK, TQ), BF16),
+    sbuf=pltpu.VMEM((3, BLK, TQ), F32), pbuf=pltpu.VMEM((2, BLK, TQ), BF16), mbuf=pltpu.VMEM((2, BLK, TQ), BF16),
     ct=pltpu.VMEM((128, TQ), F32), from_prev=pltpu.VMEM((8, TQ), F32), scale=pltpu.VMEM((TQ, 128), F32),
     teach=pltpu.VMEM((HG, BLK, 128), BF16), student=pltpu.VMEM((HG, BLK, 128), BF16),
     err=pltpu.VMEM((8, BLK), F32), err_pair=pltpu.VMEM((2, 4, BLK), F32),

time: 61.4 us -> 61 us (level)
  no operation moved by 1% of the time
where the time goes in v5:
time: 61 us; the launch traced here: 60.8 us
  Pallas kernels  58.5 us (96%)
  local copies, waits for them, and re-layouts  1.58 us (3%)
  between operations  0.65 us (1%)
    pallas_call x1, Pallas kernels, on_device(): pl.pallas_call(kernel, out_shape=(pltpu.VMEM(shapes[0].shape, BF16), shap...  58.5 us
    unnamed x4, local copies, waits for them, and re-layouts  1.58 us

profile of v5, /device:TPU:89, one launch (start us, length us, event | category | flops | bytes accessed | tf_op | source)
XLA Modules:
  0.0 60.8 jit_solution(4729175812727710121)
XLA Ops:
  0.6 58.5 %shard_map.95 = (bf16[2,32,8192]{2,1,0:T(8,128)(2,1)S(1)}, f32[2,4,512]{2,1,0:T(4,128)}) custom-call(bf16[2,2048,128]{2,1,0:T(8,128)(2,1)} %bitcast.9, bf16[2,4096,128]{2,1,0:T(8,128)(2,1)} %bitcast.5, bf16[2,4096,128]{2,1,0:T(8,128)(2,1)} %bitcast.6, bf16[2,4096,128]{2,1,0:T(8,128)(2,1)} %bitcast.7, bf16[2,4096,128]{2,1,0:T(8,128)(2,1)} %bitcast.8, ...), custom_call_target="tpu_custom_call" | custom-call | flops 10000000000 | bytes 10000000 | tf_op jit(solution)/shard_map/pallas_call | solution.py:633
  59.2 0.0 copy-start
  59.2 1.0 %copy.12 = bf16[2,32,8192]{2,1,0:T(8,128)(2,1)} copy(bf16[2,32,8192]{2,1,0:T(8,128)(2,1)S(1)} %get-tuple-element.2) | data formatting | bytes 2097152
  60.2 0.0 copy-done
  60.2 0.6 copy.13
Async XLA Ops:
  59.2 1.0 %copy-start = (f32[2,4,512]{2,1,0:T(4,128)S(1)}, f32[2,4,512]{2,1,0:T(4,128)}, u32[]{:S(2)}) copy-start(f32[2,4,512]{2,1,0:T(4,128)} %get-tuple-element.7) | copy-start | bytes 49156

commit v6 on v5

--- a/solution.py
+++ b/solution.py
@@ -171,7 +171,7 @@
 
     for i in range(4):
         loads[i].wait()
-        r.wide[...] = r.raw[i].astype(F32)
+        r.wide[0:4096, :] = r.raw[i].astype(F32)
         if i < 3:
             r.kvb[0, i] = r.wide[pl.ds(w.g, BLK, stride=8), :].astype(BF16)
             if i == 0:
@@ -536,7 +536,7 @@
 DMA = pltpu.SemaphoreType.DMA
 SCRATCH = dict(
     qraw=pltpu.VMEM((2, 2048, 128), BF16), decay_raw=pltpu.VMEM((2, 4, BLK), F32),
-    raw=pltpu.VMEM((4, 4096, 128), BF16), wide=pltpu.VMEM((4096, 128), F32),
+    raw=pltpu.VMEM((4, 4096, 128), BF16), wide=pltpu.VMEM((4104, 128), F32),
     q=pltpu.VMEM((HG, BLK, 128), BF16), kvb=pltpu.VMEM((SLOTS, 3, BLK, 128), BF16),
     aux=pltpu.VMEM((SLOTS, 16, BLK), F32), outer_own=pltpu.VMEM((BLK, 128), BF16),
     csum=pltpu.VMEM((8, BLK), F32), csum_col=pltpu.VMEM((BLK, 128), F32), docq=pltpu.VMEM((8, BLK), F32),

time: 61 us -> 61 us (level)
  no operation moved by 1% of the time
where the time goes in v6:
time: 61 us; the launch traced here: 60.8 us
  Pallas kernels  58.6 us (96%)
  local copies, waits for them, and re-layouts  1.58 us (3%)
  between operations  0.65 us (1%)
    pallas_call x1, Pallas kernels, on_device(): pl.pallas_call(kernel, out_shape=(pltpu.VMEM(shapes[0].shape, BF16), shap...  58.6 us
    unnamed x4, local copies, waits for them, and re-layouts  1.58 us

profile of v6, /device:TPU:89, one launch (start us, length us, event | category | flops | bytes accessed | tf_op | source)
XLA Modules:
  0.0 60.8 jit_solution(13128532345888298689)
XLA Ops:
  0.6 58.6 %shard_map.95 = (bf16[2,32,8192]{2,1,0:T(8,128)(2,1)S(1)}, f32[2,4,512]{2,1,0:T(4,128)}) custom-call(bf16[2,2048,128]{2,1,0:T(8,128)(2,1)} %bitcast.9, bf16[2,4096,128]{2,1,0:T(8,128)(2,1)} %bitcast.5, bf16[2,4096,128]{2,1,0:T(8,128)(2,1)} %bitcast.6, bf16[2,4096,128]{2,1,0:T(8,128)(2,1)} %bitcast.7, bf16[2,4096,128]{2,1,0:T(8,128)(2,1)} %bitcast.8, ...), custom_call_target="tpu_custom_call" | custom-call | flops 10000000000 | bytes 10000000 | tf_op jit(solution)/shard_map/pallas_call | solution.py:633
  59.2 0.0 copy-start
  59.2 1.0 %copy.12 = bf16[2,32,8192]{2,1,0:T(8,128)(2,1)} copy(bf16[2,32,8192]{2,1,0:T(8,128)(2,1)S(1)} %get-tuple-element.2) | data formatting | bytes 2097152
  60.2 0.0 copy-done
  60.2 0.6 copy.13
Async XLA Ops:
  59.2 1.0 %copy-start = (f32[2,4,512]{2,1,0:T(4,128)S(1)}, f32[2,4,512]{2,1,0:T(4,128)}, u32[]{:S(2)}) copy-start(f32[2,4,512]{2,1,0:T(4,128)} %get-tuple-element.7) | copy-start | bytes 49156
